TPU v7x, 512 devices: a whole 4x8x8 slice. The times are simulated.
512 devices in a mesh: dp: 16 (over y, x_hi), seq: 32 (over x_lo, z, core).
Axes of the slice: x: 4 (x_hi: 2, x_lo: 2; x = x_hi * 2 + x_lo), y: 8, z: 8, core: 2. Of those that a mesh axis runs over, the one named last changes fastest.
Arguments:
- queries: bfloat16 [32, 32, 128, 1152], P('dp', 'seq'), may hold values from -15 to 15
- key_states: bfloat16 [32, 32, 128, 1152], P('dp', 'seq'), may hold values from -8 to 8
- value_states: bfloat16 [32, 32, 128, 1152], P('dp', 'seq'), may hold values from -6 to 6
- gate_vector: float32 [32, 1152], P('dp'), may hold values from 0.5 to 2
- out_weight: bfloat16 [1152, 1152], P('seq'), may hold values from -0.1875 to 0.1875
- cotangent: bfloat16 [32, 32, 128, 1152], P('dp', None, 'seq'), may hold values from -6 to 6
Outputs:
- branch: bfloat16 [32, 32, 128, 1152], P('dp', None, 'seq')
- grad_query: bfloat16 [32, 32, 128, 1152], P('dp', 'seq')
- grad_key: bfloat16 [32, 32, 128, 1152], P('dp', 'seq')
- grad_value: bfloat16 [32, 32, 128, 1152], P('dp', 'seq')
- grad_weight: float32 [1152, 1152], P('seq')
All inputs are finite; a program needn't handle non-finite values.
Results may differ from a plain program's by a relative error of at most 0.023.
Values may be sent and summed in bfloat16 or wider, within the bound.
A program may use at most 64 MiB of HBM per device.

v0:
```python
import math

import jax
import jax.numpy as jnp
from jax import lax
from jax.sharding import PartitionSpec as P

HEADS = 16


def split_heads(tensor):
    return tensor.reshape(tensor.shape[:-1] + (HEADS, tensor.shape[-1] // HEADS))


def softmax_weights(queries, key_states):
    scaling = 1.0 / math.sqrt(queries.shape[-1] // HEADS)
    scores = (
        jnp.einsum(
            "cfxhd,cgxhd->cxhfg",
            split_heads(queries),
            split_heads(key_states),
            preferred_element_type=jnp.float32,
        )
        * scaling
    )
    return jax.nn.softmax(scores, axis=-1)


def attend(queries, key_states, value_states):
    weights = softmax_weights(queries, key_states).astype(jnp.bfloat16)
    heads_out = jnp.einsum(
        "cxhfg,cgxhd->cfxhd", weights, split_heads(value_states), preferred_element_type=jnp.float32
    )
    return heads_out.reshape(queries.shape).astype(jnp.bfloat16)


def attend_back(queries, key_states, value_states, attended_grad):
    scaling = 1.0 / math.sqrt(queries.shape[-1] // HEADS)
    probability = softmax_weights(queries, key_states)
    weights = probability.astype(jnp.bfloat16)
    grad_heads = split_heads(attended_grad)
    weight_grad = jnp.einsum(
        "cfxhd,cgxhd->cxhfg",
        grad_heads,
        split_heads(value_states),
        preferred_element_type=jnp.float32,
    )
    centred = weight_grad - jnp.sum(probability * weight_grad, axis=-1, keepdims=True)
    score_grad = (probability * centred * scaling).astype(jnp.bfloat16)
    query_grad = jnp.einsum(
        "cxhfg,cgxhd->cfxhd",
        score_grad,
        split_heads(key_states),
        preferred_element_type=jnp.float32,
    )
    key_grad = jnp.einsum(
        "cxhfg,cfxhd->cgxhd", score_grad, split_heads(queries), preferred_element_type=jnp.float32
    )
    value_grad = jnp.einsum(
        "cxhfg,cfxhd->cgxhd", weights, grad_heads, preferred_element_type=jnp.float32
    )
    return tuple(
        (
            tensor.reshape(queries.shape).astype(jnp.bfloat16)
            for tensor in (query_grad, key_grad, value_grad)
        )
    )


def body(queries, key_states, value_states, gate_vector, out_weight, cotangent):
    query_local, key_local, value_local = (
        lax.all_to_all(queries, "seq", split_axis=2, concat_axis=1, tiled=True),
        lax.all_to_all(key_states, "seq", split_axis=2, concat_axis=1, tiled=True),
        lax.all_to_all(value_states, "seq", split_axis=2, concat_axis=1, tiled=True),
    )
    attended = attend(query_local, key_local, value_local)
    row_count = attended.shape[0] * attended.shape[1] * attended.shape[2]
    feature_count = attended.shape[3]
    flat_attended = attended.reshape(row_count, feature_count)
    gate_wide = gate_vector[:, None, None, :]
    mixed_grad = (
        (gate_wide * cotangent.astype(jnp.float32))
        .astype(jnp.bfloat16)
        .reshape(row_count, feature_count)
    )
    projected = lax.dot_general(
        flat_attended,
        lax.all_gather(out_weight, "seq", axis=0, tiled=True),
        (((1,), (1,)), ((), ())),
        preferred_element_type=jnp.float32,
    )
    columns = mixed_grad
    attended_grad = jnp.dot(
        columns,
        lax.all_gather(out_weight, "seq", axis=0, tiled=True),
        preferred_element_type=jnp.float32,
    )
    branch = (gate_wide * projected.reshape(attended.shape)).astype(jnp.bfloat16)
    query_grad, key_grad, value_grad = attend_back(
        query_local,
        key_local,
        value_local,
        attended_grad.astype(jnp.bfloat16).reshape(attended.shape),
    )
    grad_query, grad_key, grad_value = (
        lax.all_to_all(query_grad, "seq", split_axis=1, concat_axis=2, tiled=True),
        lax.all_to_all(key_grad, "seq", split_axis=1, concat_axis=2, tiled=True),
        lax.all_to_all(value_grad, "seq", split_axis=1, concat_axis=2, tiled=True),
    )
    token_count = row_count * lax.axis_size("dp") * lax.axis_size("seq")
    inverse_root = 1.0 / math.sqrt(token_count)
    columns = mixed_grad
    seq_sum = lax.psum_scatter(
        (
            lax.dot_general(
                columns, flat_attended, (((0,), (0,)), ((), ())), preferred_element_type=jnp.float32
            )
            * inverse_root
        ).astype(jnp.bfloat16),
        "seq",
        scatter_dimension=0,
        tiled=True,
    ).astype(jnp.float32)
    grad_weight = lax.psum(seq_sum, "dp")
    return (branch, grad_query, grad_key, grad_value, grad_weight)


def solution(mesh):
    placed = (
        P("dp", "seq", None, None),
        P("dp", "seq", None, None),
        P("dp", "seq", None, None),
        P("dp", None),
        P("seq", None),
        P("dp", None, "seq", None),
    )
    return jax.shard_map(
        body,
        mesh=mesh,
        in_specs=placed,
        out_specs=(
            P("dp", None, "seq", None),
            P("dp", "seq", None, None),
            P("dp", "seq", None, None),
            P("dp", "seq", None, None),
            P("seq", None),
        ),
        check_vma=False,
    )
```

profile of v0, /device:TPU:64, one launch (start us, length us, event | category | flops | bytes accessed | tf_op | source)
XLA Modules:
  0.0 477.2 jit_solution(14601554043583214819)
XLA Ops:
  11.3 11.1 %all-to-all-start = ((bf16[2,1,128,1152]{3,0,1,2:T(2,128)(2,1)}), bf16[2,1,128,1152]{3,0,1,2:T(2,128)(2,1)S(1)}, u32[]{:S(2)}, u32[]{:S(2)}) async-start(bf16[2,1,128,1152]{3,0,1,2:T(2,128)(2,1)} %copy.89), calls=%async_computation | async-start | bytes 1179648 | tf_op jit(solution)/shard_map/all_to_all | solution.py:72
  23.8 19.8 %all-to-all-done = bf16[2,1,128,1152]{3,0,1,2:T(2,128)(2,1)S(1)} async-done(((bf16[2,1,128,1152]{3,0,1,2:T(2,128)(2,1)}), bf16[2,1,128,1152]{3,0,1,2:T(2,128)(2,1)S(1)}, u32[]{:S(2)}, u32[]{:S(2)}) %all-to-all-start) | async-done | bytes 589856 | tf_op jit(solution)/shard_map/all_to_all | solution.py:72
  43.6 4.6 all-to-all-start.1
  49.6 21.4 %all-to-all-done.1 = bf16[2,1,128,1152]{3,0,1,2:T(2,128)(2,1)S(1)} async-done(((bf16[2,1,128,1152]{3,0,1,2:T(2,128)(2,1)}), bf16[2,1,128,1152]{3,0,1,2:T(2,128)(2,1)S(1)}, u32[]{:S(2)}, u32[]{:S(2)}) %all-to-all-start.1) | async-done | bytes 589856 | tf_op jit(solution)/shard_map/all_to_all | solution.py:73
  71.0 4.3 all-to-all-start.2
  82.0 14.2 %all-to-all-done.2 = bf16[2,1,128,1152]{3,0,1,2:T(2,128)(2,1)S(1)} async-done(((bf16[2,1,128,1152]{3,0,1,2:T(2,128)(2,1)}), bf16[2,1,128,1152]{3,0,1,2:T(2,128)(2,1)S(1)}, u32[]{:S(2)}, u32[]{:S(2)}) %all-to-all-start.2) | async-done | bytes 589856 | tf_op jit(solution)/shard_map/all_to_all | solution.py:74
  98.3 4.4 fusion.65
  102.8 5.2 %reshape.70 = bf16[1152,1152]{1,0:T(8,128)(2,1)} reshape(bf16[32,36,1152]{2,1,0:T(8,128)(2,1)} %all-gather.3.cloned.1.call-done) | data formatting | bytes 5308416
  115.2 5.8 %fusion.30 = bf16[2,32,4,16,72]{4,1,3,2,0:T(8,128)(2,1)} fusion(f32[2,4,16,32,32]{3,4,2,1,0:T(8,128)} %fusion.36, bf16[2,32,4,16,72]{4,3,0,2,1:T(8,128)(2,1)S(1)} %copy-done.4, f32[2,4,16,32,32]{3,4,2,1,0:T(8,128)} %get-tuple-element.31, f32[2,4,16,32]{3,2,1,0:T(8,128)S(1)} %get-tuple-element.30), kind=kOutput, calls=%fused_computation.24 | convolution fusion | flops 20090912 | bytes 2244608 | tf_op jit(solution)/shard_map/cxhfg,cgxhd->cfxhd/dot_general | solution.py:50
  125.2 4.4 all-to-all-start.3
  129.6 6.1 %fusion.27 = bf16[2,32,4,16,72]{4,1,3,2,0:T(8,128)(2,1)} fusion(f32[2,4,16,32,32]{3,4,2,1,0:T(8,128)} %fusion.36, bf16[2,32,4,16,72]{4,3,0,2,1:T(8,128)(2,1)} %copy-done.3, f32[2,4,16,32,32]{3,4,2,1,0:T(8,128)} %get-tuple-element.31, f32[2,4,16,32]{3,2,1,0:T(8,128)S(1)} %get-tuple-element.30), kind=kOutput, calls=%fused_computation.23 | convolution fusion | flops 20090912 | bytes 2244608 | tf_op jit(solution)/shard_map/cxhfg,cfxhd->cgxhd/dot_general | solution.py:56
  139.9 8.7 %all-to-all-done.3 = bf16[2,32,4,1152]{3,2,0,1:T(4,128)(2,1)} async-done(((bf16[2,32,4,1152]{3,2,0,1:T(4,128)(2,1)}), bf16[2,32,4,1152]{3,2,0,1:T(4,128)(2,1)}, u32[]{:S(2)}, u32[]{:S(2)}) %all-to-all-start.3) | async-done | bytes 589856 | tf_op jit(solution)/shard_map/all_to_all | solution.py:106
  148.6 4.3 all-to-all-start.4
  158.0 3.7 fusion.4
  165.5 6.7 %all-to-all-done.4 = bf16[2,32,4,1152]{3,2,0,1:T(4,128)(2,1)S(1)} async-done(((bf16[2,32,4,1152]{3,2,0,1:T(4,128)(2,1)}), bf16[2,32,4,1152]{3,2,0,1:T(4,128)(2,1)S(1)}, u32[]{:S(2)}, u32[]{:S(2)}) %all-to-all-start.4) | async-done | bytes 589856 | tf_op jit(solution)/shard_map/all_to_all | solution.py:107
  172.2 5.0 %all-to-all-start.5 = ((bf16[2,32,4,1152]{3,2,0,1:T(4,128)(2,1)}), bf16[2,32,4,1152]{3,2,0,1:T(4,128)(2,1)}, u32[]{:S(2)}, u32[]{:S(2)}) async-start(bf16[2,32,4,1152]{3,2,0,1:T(4,128)(2,1)} %reshape.76), calls=%async_computation.5 | async-start | bytes 1179648 | tf_op jit(solution)/shard_map/all_to_all | solution.py:108
  177.2 71.3 %fusion = bf16[48,1152]{1,0:T(8,128)(2,1)} fusion(bf16[1152,1152]{1,0:T(8,128)(2,1)} %fusion.4), kind=kCustom, calls=%all-reduce-scatter | all-reduce-scatter fusion | flops 1769473 | bytes 2766848
  250.4 8.4 %collective-permute-start.5 = (bf16[48,1152]{1,0:T(8,128)(2,1)}, bf16[48,1152]{1,0:T(8,128)(2,1)}, u32[]{:S(2)}, u32[]{:S(2)}) collective-permute-start(bf16[48,1152]{1,0:T(8,128)(2,1)} %fusion), channel_id=1, source_target_pairs={{0,6},{1,7},{2,8},{3,9},{4,10},{5,11},{6,12},{7,13},{8,14},{9,15},... | collective-permute-start | bytes 331784
  259.7 5.5 %collective-permute-start.7 = (bf16[36,1152]{1,0:T(8,128)(2,1)S(1)}, bf16[36,1152]{1,0:T(8,128)(2,1)S(1)}, u32[]{:S(2)}, u32[]{:S(2)}) collective-permute-start(bf16[36,1152]{1,0:T(8,128)(2,1)S(1)} %slice), channel_id=1, source_target_pairs={{0,8},{1,9},{2,10},{3,11},{4,12},{5,13},{6,14},{7,15},{8,16},{9,17... | collective-permute-start | bytes 248840
  269.8 4.8 collective-permute-start.2
  274.5 4.7 collective-permute-start.1
  279.2 4.7 collective-permute-start
  288.5 14.5 %concatenate = bf16[420,1152]{1,0:T(8,128)(2,1)} concatenate(bf16[36,1152]{1,0:T(8,128)(2,1)} %copy-done.8, bf16[48,1152]{1,0:T(8,128)(2,1)} %collective-permute-done.6, bf16[48,1152]{1,0:T(8,128)(2,1)} %collective-permute-done.5, bf16[48,1152]{1,0:T(8,128)(2,1)} %collective-permute-done.4, bf16[48,1152]{1,0:T(8,128)(2,1)} %collective-permute-done.3, ...), dimensions={0} | concatenate | bytes 1935360
  317.1 151.0 %all-reduce.4.cloned.1.call-done = f32[36,1152]{1,0:T(8,128)} async-done(((f32[36,1152]{1,0:T(8,128)}), f32[36,1152]{1,0:T(8,128)}) %all-reduce.4.cloned.1.call-update) | async-done | bytes 165904 | tf_op jit(solution)/shard_map/psum | solution.py:124
  (78 shorter events, 66.1 us)
Async XLA Ops:
  8.0 14.4 %copy-start.5 = (bf16[2,1,128,1152]{3,2,1,0:T(8,128)(2,1)S(1)}, bf16[2,1,128,1152]{3,2,1,0:T(8,128)(2,1)}, u32[]{:S(2)}) copy-start(bf16[2,1,128,1152]{3,2,1,0:T(8,128)(2,1)} %param.7) | copy-start | bytes 1769476
  8.0 94.8 %all-gather.3.cloned.1.call-start = ((), (), s32[]{:S(2)}) async-start(), calls=%async_computation.7 | async-start | bytes 3041280 | tf_op jit(solution)/shard_map/all_gather | solution.py:88
  8.7 39.5 %copy-start.6 = (bf16[2,1,128,1152]{3,2,1,0:T(8,128)(2,1)S(1)}, bf16[2,1,128,1152]{3,2,1,0:T(8,128)(2,1)}, u32[]{:S(2)}) copy-start(bf16[2,1,128,1152]{3,2,1,0:T(8,128)(2,1)} %param.8) | copy-start | bytes 1769476
  11.3 32.3 %all-to-all-start = ((bf16[2,1,128,1152]{3,0,1,2:T(2,128)(2,1)}), bf16[2,1,128,1152]{3,0,1,2:T(2,128)(2,1)S(1)}, u32[]{:S(2)}, u32[]{:S(2)}) async-start(bf16[2,1,128,1152]{3,0,1,2:T(2,128)(2,1)} %copy.89), calls=%async_computation | async-start | bytes 1179648 | tf_op jit(solution)/shard_map/all_to_all | solution.py:72
  22.4 53.0 %copy-start.7 = (bf16[2,32,4,1152]{3,2,1,0:T(4,128)(2,1)S(1)}, bf16[2,32,4,1152]{3,2,1,0:T(4,128)(2,1)}, u32[]{:S(2)}) copy-start(bf16[2,32,4,1152]{3,2,1,0:T(4,128)(2,1)} %param.11) | copy-start | bytes 1769476
  22.4 53.0 %copy-start.9 = (f32[2,1152]{1,0:T(2,128)S(1)}, f32[2,1152]{1,0:T(2,128)}, u32[]{:S(2)}) copy-start(f32[2,1152]{1,0:T(2,128)} %param.9) | copy-start | bytes 27652
  43.6 27.5 %all-to-all-start.1 = ((bf16[2,1,128,1152]{3,0,1,2:T(2,128)(2,1)}), bf16[2,1,128,1152]{3,0,1,2:T(2,128)(2,1)S(1)}, u32[]{:S(2)}, u32[]{:S(2)}) async-start(bf16[2,1,128,1152]{3,0,1,2:T(2,128)(2,1)} %copy.91), calls=%async_computation.1 | async-start | bytes 1179648 | tf_op jit(solution)/shard_map/all_to_all | solution.py:73
  71.0 25.2 %all-to-all-start.2 = ((bf16[2,1,128,1152]{3,0,1,2:T(2,128)(2,1)}), bf16[2,1,128,1152]{3,0,1,2:T(2,128)(2,1)S(1)}, u32[]{:S(2)}, u32[]{:S(2)}) async-start(bf16[2,1,128,1152]{3,0,1,2:T(2,128)(2,1)} %copy.95), calls=%async_computation.2 | async-start | bytes 1179648 | tf_op jit(solution)/shard_map/all_to_all | solution.py:74
  78.9 23.9 %copy-start.3 = (bf16[2,32,4,16,72]{4,3,0,2,1:T(8,128)(2,1)}, bf16[2,32,4,16,72]{4,3,0,2,1:T(8,128)(2,1)S(1)}, u32[]{:S(2)}) copy-start(bf16[2,32,4,16,72]{4,3,0,2,1:T(8,128)(2,1)S(1)} %reshape.78) | copy-start | bytes 1769476
  102.8 26.8 %copy-start.11 = (f32[2,4,16,32]{3,2,1,0:T(8,128)}, f32[2,4,16,32]{3,2,1,0:T(8,128)S(1)}, u32[]{:S(2)}) copy-start(f32[2,4,16,32]{3,2,1,0:T(8,128)S(1)} %get-tuple-element.30) | copy-start | bytes 49156
  125.2 23.4 %all-to-all-start.3 = ((bf16[2,32,4,1152]{3,2,0,1:T(4,128)(2,1)}), bf16[2,32,4,1152]{3,2,0,1:T(4,128)(2,1)}, u32[]{:S(2)}, u32[]{:S(2)}) async-start(bf16[2,32,4,1152]{3,2,0,1:T(4,128)(2,1)} %reshape.74), calls=%async_computation.3 | async-start | bytes 1179648 | tf_op jit(solution)/shard_map/all_to_all | solution.py:106
  148.6 23.6 %all-to-all-start.4 = ((bf16[2,32,4,1152]{3,2,0,1:T(4,128)(2,1)}), bf16[2,32,4,1152]{3,2,0,1:T(4,128)(2,1)S(1)}, u32[]{:S(2)}, u32[]{:S(2)}) async-start(bf16[2,32,4,1152]{3,2,0,1:T(4,128)(2,1)} %reshape.75), calls=%async_computation.4 | async-start | bytes 1179648 | tf_op jit(solution)/shard_map/all_to_all | solution.py:107
  158.0 3.7 copy-start.12
  172.2 142.5 %all-to-all-start.5 = ((bf16[2,32,4,1152]{3,2,0,1:T(4,128)(2,1)}), bf16[2,32,4,1152]{3,2,0,1:T(4,128)(2,1)}, u32[]{:S(2)}, u32[]{:S(2)}) async-start(bf16[2,32,4,1152]{3,2,0,1:T(4,128)(2,1)} %reshape.76), calls=%async_computation.5 | async-start | bytes 1179648 | tf_op jit(solution)/shard_map/all_to_all | solution.py:108
  177.1 127.5 %copy-start = (bf16[32,36,1152]{2,1,0:T(8,128)(2,1)S(1)}, bf16[32,36,1152]{2,1,0:T(8,128)(2,1)}, u32[]{:S(2)}) copy-start(bf16[32,36,1152]{2,1,0:T(8,128)(2,1)} %all-gather.3.cloned.1.call-done) | copy-start | bytes 7962628
  177.1 291.0 %all-reduce.4.cloned.1.call-start = ((), (), s32[]{:S(2)}) async-start(), calls=%async_computation.6 | async-start | bytes 368640 | tf_op jit(solution)/shard_map/psum | solution.py:124
  248.5 26.0 %collective-permute-start.6 = (bf16[48,1152]{1,0:T(8,128)(2,1)}, bf16[48,1152]{1,0:T(8,128)(2,1)}, u32[]{:S(2)}, u32[]{:S(2)}) collective-permute-start(bf16[48,1152]{1,0:T(8,128)(2,1)} %fusion), channel_id=1, source_target_pairs={{0,7},{1,8},{2,9},{3,10},{4,11},{5,12},{6,13},{7,14},{8,15},{9,16}... | collective-permute-start | bytes 331784
  250.4 28.8 %collective-permute-start.5 = (bf16[48,1152]{1,0:T(8,128)(2,1)}, bf16[48,1152]{1,0:T(8,128)(2,1)}, u32[]{:S(2)}, u32[]{:S(2)}) collective-permute-start(bf16[48,1152]{1,0:T(8,128)(2,1)} %fusion), channel_id=1, source_target_pairs={{0,6},{1,7},{2,8},{3,9},{4,10},{5,11},{6,12},{7,13},{8,14},{9,15},... | collective-permute-start | bytes 331784
  259.7 9.4 %collective-permute-start.7 = (bf16[36,1152]{1,0:T(8,128)(2,1)S(1)}, bf16[36,1152]{1,0:T(8,128)(2,1)S(1)}, u32[]{:S(2)}, u32[]{:S(2)}) collective-permute-start(bf16[36,1152]{1,0:T(8,128)(2,1)S(1)} %slice), channel_id=1, source_target_pairs={{0,8},{1,9},{2,10},{3,11},{4,12},{5,13},{6,14},{7,15},{8,16},{9,17... | collective-permute-start | bytes 248840
  265.2 20.6 %collective-permute-start.4 = (bf16[48,1152]{1,0:T(8,128)(2,1)}, bf16[48,1152]{1,0:T(8,128)(2,1)}, u32[]{:S(2)}, u32[]{:S(2)}) collective-permute-start(bf16[48,1152]{1,0:T(8,128)(2,1)} %fusion), channel_id=1, source_target_pairs={{0,5},{1,6},{2,7},{3,8},{4,9},{5,10},{6,11},{7,12},{8,13},{9,14},{... | collective-permute-start | bytes 331784
  267.2 18.7 %collective-permute-start.3 = (bf16[48,1152]{1,0:T(8,128)(2,1)}, bf16[48,1152]{1,0:T(8,128)(2,1)}, u32[]{:S(2)}, u32[]{:S(2)}) collective-permute-start(bf16[48,1152]{1,0:T(8,128)(2,1)} %fusion), channel_id=1, source_target_pairs={{0,4},{1,5},{2,6},{3,7},{4,8},{5,9},{6,10},{7,11},{8,12},{9,13},{1... | collective-permute-start | bytes 331784
  269.8 16.1 %collective-permute-start.2 = (bf16[48,1152]{1,0:T(8,128)(2,1)}, bf16[48,1152]{1,0:T(8,128)(2,1)}, u32[]{:S(2)}, u32[]{:S(2)}) collective-permute-start(bf16[48,1152]{1,0:T(8,128)(2,1)} %fusion), channel_id=1, source_target_pairs={{0,3},{1,4},{2,5},{3,6},{4,7},{5,8},{6,9},{7,10},{8,11},{9,12},{10... | collective-permute-start | bytes 331784
  274.5 12.7 %collective-permute-start.1 = (bf16[48,1152]{1,0:T(8,128)(2,1)}, bf16[48,1152]{1,0:T(8,128)(2,1)}, u32[]{:S(2)}, u32[]{:S(2)}) collective-permute-start(bf16[48,1152]{1,0:T(8,128)(2,1)} %fusion), channel_id=1, source_target_pairs={{0,2},{1,3},{2,4},{3,5},{4,6},{5,7},{6,8},{7,9},{8,10},{9,11},{10,... | collective-permute-start | bytes 331784
  279.2 9.3 %collective-permute-start = (bf16[48,1152]{1,0:T(8,128)(2,1)}, bf16[48,1152]{1,0:T(8,128)(2,1)}, u32[]{:S(2)}, u32[]{:S(2)}) collective-permute-start(bf16[48,1152]{1,0:T(8,128)(2,1)} %fusion), channel_id=1, source_target_pairs={{0,1},{1,2},{2,3},{3,4},{4,5},{5,6},{6,7},{7,8},{8,9},{9,10},{10,1... | collective-permute-start | bytes 331784
  (5 other events, 10.4 us)
Sparse Core Ops, SparseCore 0:
  11.0 79.6 all-gather.2
Sparse Core Ops, SparseCore 1:
  304.7 163.4 all-reduce.3
where the time goes:
time: 479 us; the launch traced here: 477 us
  waiting for transfers between devices  225 us (47%)
  blocking collectives  71.3 us (15%)
  starting transfers between devices  67.5 us (14%)
  local copies, waits for them, and re-layouts  63.2 us (13%)
  matrix products  31.9 us (7%)
  between operations  16.5 us (3%)
    psum x1, waiting for transfers between devices, body(): grad_weight = lax.psum(seq_sum, 'dp')  151 us
    unnamed x1, blocking collectives  71.3 us
    unnamed x39, local copies, waits for them, and re-layouts  36.4 us
    unnamed x8, starting transfers between devices  33.8 us
    all_to_all x1, waiting for transfers between devices, body(): lax.all_to_all(key_states, 'seq', split_axis=2, concat_axis=1, tiled=True)  21.4 us
    all_to_all x1, waiting for transfers between devices, body(): lax.all_to_all(queries, 'seq', split_axis=2, concat_axis=1, tiled=True)  19.8 us
    all_to_all x1, waiting for transfers between devices, body(): lax.all_to_all(value_states, 'seq', split_axis=2, concat_axis=1, tiled=True)  14.2 us
    convert_element_type x6, local copies, waits for them, and re-layouts, attend_back(): tensor.reshape(queries.shape).astype(jnp.bfloat16)  11.2 us
  transfers between devices with their start and end apart: 16, of which 8 were waited for; matrix products, arithmetic and copies ran while one was open for 30% of the time, Pallas kernels for 0%

commit v1 on v0

--- a/solution.py
+++ b/solution.py
@@ -1,11 +1,104 @@
+import functools
 import math
 
 import jax
 import jax.numpy as jnp
 from jax import lax
+from jax.experimental import pallas as pl
+from jax.experimental.pallas import tpu as pltpu
 from jax.sharding import PartitionSpec as P
 
 HEADS = 16
+
+
+MESH = pl.DeviceIdType.MESH
+
+
+def exchange_kernel(count, peers, *refs):
+    ins, outs = refs[:count], refs[count : 2 * count]
+    send_sem, recv_sem, own_sem = refs[2 * count :]
+    dp, me = lax.axis_index("dp"), lax.axis_index("seq")
+    barrier = pltpu.get_barrier_semaphore()
+
+    def greet(step, carry):
+        pl.semaphore_signal(
+            barrier, inc=1, device_id=(dp, lax.rem(me + step, peers)), device_id_type=MESH
+        )
+        return carry
+
+    lax.fori_loop(1, peers, greet, 0)
+    pl.semaphore_wait(barrier, peers - 1)
+    for t in range(count):
+
+        def send(step, carry):
+            target = lax.rem(me + step, peers)
+            pltpu.make_async_remote_copy(
+                src_ref=ins[t].at[target],
+                dst_ref=outs[t].at[me],
+                send_sem=send_sem.at[t],
+                recv_sem=recv_sem.at[t],
+                device_id=(dp, target),
+                device_id_type=MESH,
+            ).start()
+            return carry
+
+        lax.fori_loop(1, peers, send, 0)
+        pltpu.make_async_copy(ins[t].at[me], outs[t].at[me], own_sem.at[t]).start()
+    for t in range(count):
+        pltpu.make_async_copy(ins[t].at[me], outs[t].at[me], own_sem.at[t]).wait()
+        whole = pltpu.make_async_remote_copy(
+            src_ref=ins[t].at[pl.ds(0, peers - 1)],
+            dst_ref=outs[t].at[pl.ds(0, peers - 1)],
+            send_sem=send_sem.at[t],
+            recv_sem=recv_sem.at[t],
+            device_id=(dp, lax.rem(me + 1, peers)),
+            device_id_type=MESH,
+        )
+        whole.wait_send()
+        whole.wait_recv()
+
+
+def exchange(tensors, collective_id):
+    count, peers = len(tensors), tensors[0].shape[0]
+    whole = [pl.BlockSpec(memory_space=pltpu.VMEM)] * count
+    return pl.pallas_call(
+        functools.partial(exchange_kernel, count, peers),
+        out_shape=[jax.ShapeDtypeStruct(t.shape, t.dtype) for t in tensors],
+        in_specs=whole,
+        out_specs=whole,
+        scratch_shapes=[
+            pltpu.SemaphoreType.DMA((count,)),
+            pltpu.SemaphoreType.DMA((count,)),
+            pltpu.SemaphoreType.DMA((count,)),
+        ],
+        compiler_params=pltpu.CompilerParams(
+            collective_id=collective_id, has_side_effects=True, vmem_limit_bytes=32 << 20
+        ),
+    )(*tensors)
+
+
+def to_patches(tensors, peers):
+    def planes(t):
+        clips, _, patches, width = t.shape
+        t = t.reshape(clips, peers, patches // peers, width).transpose(1, 0, 2, 3)
+        return t.reshape(peers, -1, width)
+
+    clips, _, patches, width = tensors[0].shape
+    arrived = exchange([planes(t) for t in tensors], 1)
+    return [
+        t.reshape(peers, clips, patches // peers, width).transpose(1, 0, 2, 3) for t in arrived
+    ]
+
+
+def to_frames(tensors, peers):
+    clips, _, patches, width = tensors[0].shape
+    arrived = exchange([t.transpose(1, 0, 2, 3).reshape(peers, -1, width) for t in tensors], 2)
+    return [
+        t.reshape(peers, clips, patches, width)
+        .transpose(1, 0, 2, 3)
+        .reshape(clips, 1, peers * patches, width)
+        for t in arrived
+    ]
 
 
 def split_heads(tensor):
@@ -68,11 +161,8 @@
 
 
 def body(queries, key_states, value_states, gate_vector, out_weight, cotangent):
-    query_local, key_local, value_local = (
-        lax.all_to_all(queries, "seq", split_axis=2, concat_axis=1, tiled=True),
-        lax.all_to_all(key_states, "seq", split_axis=2, concat_axis=1, tiled=True),
-        lax.all_to_all(value_states, "seq", split_axis=2, concat_axis=1, tiled=True),
-    )
+    peers = lax.axis_size("seq")
+    query_local, key_local, value_local = to_patches((queries, key_states, value_states), peers)
     attended = attend(query_local, key_local, value_local)
     row_count = attended.shape[0] * attended.shape[1] * attended.shape[2]
     feature_count = attended.shape[3]
@@ -102,11 +192,7 @@
         value_local,
         attended_grad.astype(jnp.bfloat16).reshape(attended.shape),
     )
-    grad_query, grad_key, grad_value = (
-        lax.all_to_all(query_grad, "seq", split_axis=1, concat_axis=2, tiled=True),
-        lax.all_to_all(key_grad, "seq", split_axis=1, concat_axis=2, tiled=True),
-        lax.all_to_all(value_grad, "seq", split_axis=1, concat_axis=2, tiled=True),
-    )
+    grad_query, grad_key, grad_value = to_frames((query_grad, key_grad, value_grad), peers)
     token_count = row_count * lax.axis_size("dp") * lax.axis_size("seq")
     inverse_root = 1.0 / math.sqrt(token_count)
     columns = mixed_grad

time: 479 us -> 372 us (0.78)
  waiting for transfers between devices: 225 us -> 74.1 us
  Pallas kernels: 0 us -> 106 us
  starting transfers between devices: 67.5 us -> 34.2 us
  local copies, waits for them, and re-layouts: 63.2 us -> 44.4 us
  blocking collectives: 71.3 us -> 64.4 us
    pallas_call x0 -> x2, Pallas kernels: none -> 106 us  [exchange(): pl.pallas_call(functools.partial(exchange_kernel, count, peers), out_shap...]
    psum x1, waiting for transfers between devices: 151 us -> 72.1 us  [body(): grad_weight = lax.psum(seq_sum, 'dp')]
    all_to_all x6 -> x0, waiting for transfers between devices: 70.8 us -> none  [the longest x1 21.4 us: body(): lax.all_to_all(key_states, 'seq', split_axis=2, concat_axis=1, tiled=True)]
    all_to_all x6 -> x0, starting transfers between devices: 33.6 us -> none  [the longest x1 11.1 us: body(): lax.all_to_all(queries, 'seq', split_axis=2, concat_axis=1, tiled=True)]
    unnamed x39, local copies, waits for them, and re-layouts: 36.4 us -> 18.1 us
    unnamed x1, blocking collectives: 71.3 us -> 64.4 us
    reshape x0 -> x21, local copies, waits for them, and re-layouts: none -> 6.84 us  [the longest x3 2.85 us: to_frames(): return [t.reshape(peers, clips, patches, width).transpose(1, 0, 2, 3).res...]
  transfers between devices with their start and end apart: 16 -> 10, of which waited for: 8 -> 3; matrix products, arithmetic and copies ran while one was open for 30% -> 37% of each run, Pallas kernels for 0% -> 28%
where the time goes in v1:
time: 372 us; the launch traced here: 371 us
  Pallas kernels  106 us (28%)
  waiting for transfers between devices  74.1 us (20%)
  blocking collectives  64.4 us (17%)
  local copies, waits for them, and re-layouts  44.4 us (12%)
  starting transfers between devices  34.2 us (9%)
  matrix products  30.8 us (8%)
  between operations  16.6 us (4%)
    pallas_call x2, Pallas kernels, exchange(): pl.pallas_call(functools.partial(exchange_kernel, count, peers), out_shap...  106 us
    psum x1, waiting for transfers between devices, body(): grad_weight = lax.psum(seq_sum, 'dp')  72.1 us
    unnamed x1, blocking collectives  64.4 us
    unnamed x8, starting transfers between devices  34.1 us
    unnamed x39, local copies, waits for them, and re-layouts  18.1 us
    convert_element_type x6, local copies, waits for them, and re-layouts, attend_back(): tensor.reshape(queries.shape).astype(jnp.bfloat16)  7.61 us
  transfers between devices with their start and end apart: 10, of which 3 were waited for; matrix products, arithmetic and copies ran while one was open for 37% of the time, Pallas kernels for 28%

profile of v1, /device:TPU:64, one launch (start us, length us, event | category | flops | bytes accessed | tf_op | source)
XLA Modules:
  0.0 371.1 jit_solution(7332399808933559391)
XLA Ops:
  12.1 59.5 %shard_map.101 = (bf16[32,8,1152]{2,1,0:T(8,128)(2,1)S(1)}, bf16[32,8,1152]{2,1,0:T(8,128)(2,1)S(1)}, bf16[32,8,1152]{2,1,0:T(8,128)(2,1)S(1)}) custom-call(bf16[32,8,1152]{2,1,0:T(8,128)(2,1)S(1)} %reshape.99.refs_0_, bf16[32,8,1152]{2,1,0:T(8,128)(2,1)S(1)} %reshape.101.refs_1_, bf16[32,8,1152]{2,1,0:T(8,128)(2,1)S(1)} %reshape.103.refs_2_), custom_call_target="tpu_custom_call" | custom-call | tf_op jit(solution)/shard_map/pallas_call | solution.py:64
  71.7 1.8 reshape.105
  73.6 2.8 reshape.107
  78.3 4.1 %fusion.65 = (f32[2,4,16,32]{3,2,1,0:T(8,128)S(1)}, f32[2,4,16,32,32]{3,4,2,1,0:T(8,128)}) fusion(bf16[2,32,4,16,72]{4,3,1,2,0:T(8,128)(2,1)S(1)} %reshape.109, bf16[2,32,4,16,72]{4,3,1,2,0:T(8,128)(2,1)} %reshape.107), kind=kOutput, calls=%fused_computation.51 | convolution fusion | flops 19267616 | bytes 1720320 | tf_op jit(solution)/shard_map/sub | solution.py:119
  83.0 2.2 fusion.25
  87.1 2.6 fusion.4
  89.6 64.4 %fusion = bf16[48,1152]{1,0:T(8,128)(2,1)S(1)} fusion(bf16[1152,1152]{1,0:T(8,128)(2,1)} %fusion.4), kind=kCustom, calls=%all-reduce-scatter | all-reduce-scatter fusion | flops 1769473 | bytes 2766848
  155.3 7.6 %collective-permute-start.5 = (bf16[48,1152]{1,0:T(8,128)(2,1)S(1)}, bf16[48,1152]{1,0:T(8,128)(2,1)S(1)}, u32[]{:S(2)}, u32[]{:S(2)}) collective-permute-start(bf16[48,1152]{1,0:T(8,128)(2,1)S(1)} %fusion), channel_id=1, source_target_pairs={{0,6},{1,7},{2,8},{3,9},{4,10},{5,11},{6,12},{7,13},{8,14},{9,15},... | collective-permute-start | bytes 331784
  162.9 6.2 %collective-permute-start.7 = (bf16[36,1152]{1,0:T(8,128)(2,1)S(1)}, bf16[36,1152]{1,0:T(8,128)(2,1)S(1)}, u32[]{:S(2)}, u32[]{:S(2)}) collective-permute-start(bf16[36,1152]{1,0:T(8,128)(2,1)S(1)} %slice), channel_id=1, source_target_pairs={{0,8},{1,9},{2,10},{3,11},{4,12},{5,13},{6,14},{7,15},{8,16},{9,17... | collective-permute-start | bytes 248840
  171.7 6.1 %collective-permute-start.2 = (bf16[48,1152]{1,0:T(8,128)(2,1)S(1)}, bf16[48,1152]{1,0:T(8,128)(2,1)S(1)}, u32[]{:S(2)}, u32[]{:S(2)}) collective-permute-start(bf16[48,1152]{1,0:T(8,128)(2,1)S(1)} %fusion), channel_id=1, source_target_pairs={{0,3},{1,4},{2,5},{3,6},{4,7},{5,8},{6,9},{7,10},{8,11},{9,12},{10... | collective-permute-start | bytes 331784
  177.9 5.5 %collective-permute-start.1 = (bf16[48,1152]{1,0:T(8,128)(2,1)S(1)}, bf16[48,1152]{1,0:T(8,128)(2,1)}, u32[]{:S(2)}, u32[]{:S(2)}) collective-permute-start(bf16[48,1152]{1,0:T(8,128)(2,1)S(1)} %fusion), channel_id=1, source_target_pairs={{0,2},{1,3},{2,4},{3,5},{4,6},{5,7},{6,8},{7,9},{8,10},{9,11},{10,... | collective-permute-start | bytes 331784
  183.4 4.8 %collective-permute-start = (bf16[48,1152]{1,0:T(8,128)(2,1)S(1)}, bf16[48,1152]{1,0:T(8,128)(2,1)}, u32[]{:S(2)}, u32[]{:S(2)}) collective-permute-start(bf16[48,1152]{1,0:T(8,128)(2,1)S(1)} %fusion), channel_id=1, source_target_pairs={{0,1},{1,2},{2,3},{3,4},{4,5},{5,6},{6,7},{7,8},{8,9},{9,10},{10,1... | collective-permute-start | bytes 331784
  192.8 4.6 %concatenate = bf16[420,1152]{1,0:T(8,128)(2,1)S(1)} concatenate(bf16[36,1152]{1,0:T(8,128)(2,1)} %copy-done.10, bf16[48,1152]{1,0:T(8,128)(2,1)S(1)} %collective-permute-done.6, bf16[48,1152]{1,0:T(8,128)(2,1)S(1)} %collective-permute-done.5, bf16[48,1152]{1,0:T(8,128)(2,1)S(1)} %collective-permute-done.4, bf16[48,1152]{1,0:T(8,128)(2,1)S(1)} %collective-permute-done.3, ...), dimensions={0} | concatenate | bytes 1935360
  198.1 5.2 %reshape.121 = bf16[1152,1152]{1,0:T(8,128)(2,1)} reshape(bf16[32,36,1152]{2,1,0:T(8,128)(2,1)} %all-gather.3.cloned.1.call-done) | data formatting | bytes 5308416
  203.4 2.7 convolution_convert_fusion
  206.1 1.8 reshape_reshape.3
  208.9 2.3 fusion.37
  211.2 3.2 fusion.26
  214.4 2.2 reshape.122
  216.7 2.9 fusion.6
  222.6 5.4 %fusion.27 = bf16[2,32,4,16,72]{4,1,3,2,0:T(8,128)(2,1)} fusion(f32[2,4,16,32,32]{3,4,2,1,0:T(8,128)} %fusion.37, bf16[2,32,4,16,72]{4,3,1,2,0:T(8,128)(2,1)S(1)} %copy-done.4, f32[2,4,16,32,32]{3,4,2,1,0:T(8,128)} %get-tuple-element.33, f32[2,4,16,32]{3,2,1,0:T(8,128)S(1)} %copy-done.15), kind=kOutput, calls=%fused_computation.23 | convolution fusion | flops 20090912 | bytes 2244608 | tf_op jit(solution)/shard_map/cxhfg,cfxhd->cgxhd/dot_general | solution.py:149
  231.2 5.5 %fusion.30 = bf16[2,32,4,16,72]{4,1,3,2,0:T(8,128)(2,1)} fusion(f32[2,4,16,32,32]{3,4,2,1,0:T(8,128)} %fusion.37, bf16[2,32,4,16,72]{4,3,1,2,0:T(8,128)(2,1)S(1)} %copy-done.3, f32[2,4,16,32,32]{3,4,2,1,0:T(8,128)} %get-tuple-element.33, f32[2,4,16,32]{3,2,1,0:T(8,128)S(1)} %copy-done.15), kind=kOutput, calls=%fused_computation.24 | convolution fusion | flops 20090912 | bytes 2244608 | tf_op jit(solution)/shard_map/cxhfg,cgxhd->cfxhd/dot_general | solution.py:143
  239.8 46.3 %shard_map.102 = (bf16[32,8,1152]{2,1,0:T(8,128)(2,1)S(1)}, bf16[32,8,1152]{2,1,0:T(8,128)(2,1)S(1)}, bf16[32,8,1152]{2,1,0:T(8,128)(2,1)S(1)}) custom-call(bf16[32,8,1152]{2,1,0:T(8,128)(2,1)S(1)} %copy.88.refs_0_, bf16[32,8,1152]{2,1,0:T(8,128)(2,1)S(1)} %copy.89.refs_1_, bf16[32,8,1152]{2,1,0:T(8,128)(2,1)S(1)} %copy.90.refs_2_), custom_call_target="tpu_custom_call" | custom-call | tf_op jit(solution)/shard_map/pallas_call | solution.py:64
  290.0 72.1 %all-reduce.4.cloned.1.call-done = f32[36,1152]{1,0:T(8,128)} async-done(((f32[36,1152]{1,0:T(8,128)}), f32[36,1152]{1,0:T(8,128)}) %all-reduce.4.cloned.1.call-update) | async-done | bytes 165904 | tf_op jit(solution)/shard_map/psum | solution.py:210
  (89 shorter events, 32.8 us)
Async XLA Ops:
  8.0 2.7 copy-start.6
  8.0 190.1 %all-gather.3.cloned.1.call-start = ((), (), s32[]{:S(2)}) async-start(), calls=%async_computation.1 | async-start | bytes 3041280 | tf_op jit(solution)/shard_map/all_gather | solution.py:178
  8.7 353.3 %all-reduce.4.cloned.1.call-start = ((), (), s32[]{:S(2)}) async-start(), calls=%async_computation | async-start | bytes 368640 | tf_op jit(solution)/shard_map/psum | solution.py:210
  10.6 1.1 copy-start.7
  78.3 4.1 %copy-start.2 = (bf16[2,32,4,16,72]{4,3,1,2,0:T(8,128)(2,1)}, bf16[2,32,4,16,72]{4,3,1,2,0:T(8,128)(2,1)S(1)}, u32[]{:S(2)}) copy-start(bf16[2,32,4,16,72]{4,3,1,2,0:T(8,128)(2,1)S(1)} %reshape.109) | copy-start | bytes 1769476
  85.2 1.7 copy-start.9
  85.2 1.7 copy-start.11
  154.0 23.9 %collective-permute-start.6 = (bf16[48,1152]{1,0:T(8,128)(2,1)S(1)}, bf16[48,1152]{1,0:T(8,128)(2,1)S(1)}, u32[]{:S(2)}, u32[]{:S(2)}) collective-permute-start(bf16[48,1152]{1,0:T(8,128)(2,1)S(1)} %fusion), channel_id=1, source_target_pairs={{0,7},{1,8},{2,9},{3,10},{4,11},{5,12},{6,13},{7,14},{8,15},{9,16}... | collective-permute-start | bytes 331784
  155.3 28.1 %collective-permute-start.5 = (bf16[48,1152]{1,0:T(8,128)(2,1)S(1)}, bf16[48,1152]{1,0:T(8,128)(2,1)S(1)}, u32[]{:S(2)}, u32[]{:S(2)}) collective-permute-start(bf16[48,1152]{1,0:T(8,128)(2,1)S(1)} %fusion), channel_id=1, source_target_pairs={{0,6},{1,7},{2,8},{3,9},{4,10},{5,11},{6,12},{7,13},{8,14},{9,15},... | collective-permute-start | bytes 331784
  162.9 8.8 %collective-permute-start.7 = (bf16[36,1152]{1,0:T(8,128)(2,1)S(1)}, bf16[36,1152]{1,0:T(8,128)(2,1)S(1)}, u32[]{:S(2)}, u32[]{:S(2)}) collective-permute-start(bf16[36,1152]{1,0:T(8,128)(2,1)S(1)} %slice), channel_id=1, source_target_pairs={{0,8},{1,9},{2,10},{3,11},{4,12},{5,13},{6,14},{7,15},{8,16},{9,17... | collective-permute-start | bytes 248840
  169.1 22.3 %collective-permute-start.4 = (bf16[48,1152]{1,0:T(8,128)(2,1)S(1)}, bf16[48,1152]{1,0:T(8,128)(2,1)S(1)}, u32[]{:S(2)}, u32[]{:S(2)}) collective-permute-start(bf16[48,1152]{1,0:T(8,128)(2,1)S(1)} %fusion), channel_id=1, source_target_pairs={{0,5},{1,6},{2,7},{3,8},{4,9},{5,10},{6,11},{7,12},{8,13},{9,14},{... | collective-permute-start | bytes 331784
  170.4 21.0 %collective-permute-start.3 = (bf16[48,1152]{1,0:T(8,128)(2,1)S(1)}, bf16[48,1152]{1,0:T(8,128)(2,1)S(1)}, u32[]{:S(2)}, u32[]{:S(2)}) collective-permute-start(bf16[48,1152]{1,0:T(8,128)(2,1)S(1)} %fusion), channel_id=1, source_target_pairs={{0,4},{1,5},{2,6},{3,7},{4,8},{5,9},{6,10},{7,11},{8,12},{9,13},{1... | collective-permute-start | bytes 331784
  171.7 16.5 %copy-start.10 = (bf16[36,1152]{1,0:T(8,128)(2,1)}, bf16[36,1152]{1,0:T(8,128)(2,1)S(1)}, u32[]{:S(2)}) copy-start(bf16[36,1152]{1,0:T(8,128)(2,1)S(1)} %collective-permute-done.7) | copy-start | bytes 248836
  171.7 19.7 %collective-permute-start.2 = (bf16[48,1152]{1,0:T(8,128)(2,1)S(1)}, bf16[48,1152]{1,0:T(8,128)(2,1)S(1)}, u32[]{:S(2)}, u32[]{:S(2)}) collective-permute-start(bf16[48,1152]{1,0:T(8,128)(2,1)S(1)} %fusion), channel_id=1, source_target_pairs={{0,3},{1,4},{2,5},{3,6},{4,7},{5,8},{6,9},{7,10},{8,11},{9,12},{10... | collective-permute-start | bytes 331784
  177.9 13.8 %collective-permute-start.1 = (bf16[48,1152]{1,0:T(8,128)(2,1)S(1)}, bf16[48,1152]{1,0:T(8,128)(2,1)}, u32[]{:S(2)}, u32[]{:S(2)}) collective-permute-start(bf16[48,1152]{1,0:T(8,128)(2,1)S(1)} %fusion), channel_id=1, source_target_pairs={{0,2},{1,3},{2,4},{3,5},{4,6},{5,7},{6,8},{7,9},{8,10},{9,11},{10,... | collective-permute-start | bytes 331784
  183.4 9.4 %collective-permute-start = (bf16[48,1152]{1,0:T(8,128)(2,1)S(1)}, bf16[48,1152]{1,0:T(8,128)(2,1)}, u32[]{:S(2)}, u32[]{:S(2)}) collective-permute-start(bf16[48,1152]{1,0:T(8,128)(2,1)S(1)} %fusion), channel_id=1, source_target_pairs={{0,1},{1,2},{2,3},{3,4},{4,5},{5,6},{6,7},{7,8},{8,9},{9,10},{10,1... | collective-permute-start | bytes 331784
  198.1 5.3 %copy-start.8 = (bf16[256,1152]{1,0:T(8,128)(2,1)S(1)}, bf16[256,1152]{1,0:T(8,128)(2,1)}, u32[]{:S(2)}) copy-start(bf16[256,1152]{1,0:T(8,128)(2,1)} %reshape.110) | copy-start | bytes 1769476
  208.9 2.3 copy-start.12
  208.9 2.3 copy-start.14
  211.2 3.2 copy-start
  216.7 4.0 %copy-start.5 = (bf16[2,32,4,16,72]{4,1,3,2,0:T(8,128)(2,1)S(1)}, bf16[2,32,4,16,72]{4,1,3,2,0:T(8,128)(2,1)}, u32[]{:S(2)}) copy-start(bf16[2,32,4,16,72]{4,1,3,2,0:T(8,128)(2,1)} %fusion.26) | copy-start | bytes 1769476
  220.7 1.9 copy-start.4
  220.7 1.9 copy-start.15
  228.0 3.2 copy-start.3
  (2 other events, 1.6 us)
Sparse Core Ops, SparseCore 0:
  11.0 82.0 all-gather.2
Sparse Core Ops, SparseCore 1:
  198.2 163.8 all-reduce.3

commit v2 on v0

v2 whole, which is shorter than its diff:
```python
import functools
import math

import jax
import jax.numpy as jnp
from jax import lax
from jax.experimental import pallas as pl
from jax.experimental.pallas import tpu as pltpu
from jax.sharding import PartitionSpec as P

HEADS = 16
MESH = pl.DeviceIdType.MESH
F32 = jnp.float32
BF16 = jnp.bfloat16
NT = (((1,), (1,)), ((), ()))
NN = (((1,), (0,)), ((), ()))
TN = (((0,), (0,)), ((), ()))


def dot(a, b, dims):
    return lax.dot_general(a, b, dims, preferred_element_type=F32)


def up8(n):
    return -(-n // 8) * 8


def kernel(
    n_y,
    n_z,
    tokens,
    q_in,
    k_in,
    v_in,
    dm_in,
    gate_in,
    w_in,
    branch_out,
    gq_out,
    gk_out,
    gv_out,
    gw_out,
    q_rec,
    k_rec,
    v_rec,
    q_rows,
    k_rows,
    v_rows,
    w_rec,
    w_full,
    bias,
    probs,
    d_att,
    wide,
    wide2,
    gq_send,
    gk_send,
    gv_send,
    dm_rows,
    dm_sib,
    att,
    att_sib,
    x_own,
    x_send,
    x_rec,
    x_sum,
    z_send,
    z_rec,
    y_rec,
    fin,
    a2a_send,
    a2a_recv,
    a2a_own,
    w_send,
    w_recv,
    sib_send,
    sib_recv,
    x_ssem,
    x_rsem,
    r_send,
    r_recv,
):
    peers, group, width = q_in.shape
    rows = peers * group
    head = width // HEADS
    scale = 1.0 / math.sqrt(head)
    own_rows = w_in.shape[0]
    half = own_rows // 2
    dp, seq = lax.axis_index("dp"), lax.axis_index("seq")
    y, x_hi = lax.div(dp, 2), lax.rem(dp, 2)
    core, z, x_lo = lax.rem(seq, 2), lax.rem(lax.div(seq, 2), n_z), lax.div(seq, 2 * n_z)
    x = 2 * x_hi + x_lo

    def at(y_=None, x_=None, z_=None, core_=None):
        y_ = y if y_ is None else y_
        x_ = x if x_ is None else x_
        z_ = z if z_ is None else z_
        core_ = core if core_ is None else core_
        return (2 * y_ + lax.div(x_, 2), (lax.rem(x_, 2) * n_z + z_) * 2 + core_)

    def remote(src, dst, send, recv, to):
        return pltpu.make_async_remote_copy(
            src_ref=src,
            dst_ref=dst,
            send_sem=send,
            recv_sem=recv,
            device_id=to,
            device_id_type=MESH,
        )

    sibling = at(core_=1 - core)
    ahead, behind = at(x_=lax.rem(x + 1, 4)), at(x_=lax.rem(x + 3, 4))

    barrier = pltpu.get_barrier_semaphore()

    def greet(to):
        pl.semaphore_signal(barrier, inc=1, device_id=to, device_id_type=MESH)

    def greet_seq(step, carry):
        greet((dp, lax.rem(seq + step, peers)))
        return carry

    lax.fori_loop(1, peers, greet_seq, 0)
    for step in range(1, n_y):
        greet(at(y_=lax.rem(y + step, n_y)))
    greet(at(x_=2 * (1 - x_hi)))
    greet(at(x_=2 * (1 - x_hi) + 1))
    pl.semaphore_wait(barrier, peers - 1 + n_y - 1 + 2)

    slot = lax.rem(z + y, n_z)
    w_first = remote(
        w_in,
        w_rec.at[core, x_lo, z],
        w_send.at[0],
        w_recv.at[0],
        at(z_=lax.rem(z - y + n_z, n_z)),
    )
    w_own = pltpu.make_async_copy(w_in, w_rec.at[core, x_lo, z], w_recv.at[5])

    @pl.when(y != 0)
    def _():
        w_first.start()

    @pl.when(y == 0)
    def _():
        w_own.start()

    def spread(t, src, dst):
        def send(step, carry):
            target = lax.rem(seq + step, peers)
            remote(
                src.at[target], dst.at[seq], a2a_send.at[t], a2a_recv.at[t], (dp, target)
            ).start()
            return carry

        lax.fori_loop(1, peers, send, 0)
        pltpu.make_async_copy(src.at[seq], dst.at[seq], a2a_own.at[t]).start()

    def arrive(t, src, dst):
        remote(
            src.at[pl.ds(0, peers - 1)],
            dst.at[pl.ds(0, peers - 1)],
            a2a_send.at[t],
            a2a_recv.at[t],
            sibling,
        ).wait_recv()
        pltpu.make_async_copy(src.at[seq], dst.at[seq], a2a_own.at[t]).wait()

    def sent(t, src, dst):
        remote(
            src.at[pl.ds(0, peers - 1)],
            dst.at[pl.ds(0, peers - 1)],
            a2a_send.at[t],
            a2a_recv.at[t],
            sibling,
        ).wait_send()

    spread(0, q_in, q_rec)
    spread(1, k_in, k_rec)
    spread(2, v_in, v_rec)

    block = n_z * half
    d_mixed = dm_in[...]
    row = lax.broadcasted_iota(jnp.int32, (block, 1), 0)
    turn = sum((row >= half * j).astype(jnp.int32) for j in range(1, n_z))
    row = row + turn * (2 * own_rows - half)
    lane = lax.broadcasted_iota(jnp.int32, (block, width), 1)
    for c in range(2):
        for b in range(4):
            first = (b % 2) * n_z * 2 * own_rows + c * own_rows + (b // 2) * half
            pick = (lane == row + first).astype(F32).astype(BF16)
            dm_rows[c, b] = dot(pick, d_mixed, NT).astype(BF16)
    dm_share = remote(
        dm_rows.at[1 - core], dm_sib, sib_send.at[0], sib_recv.at[0], sibling
    )
    dm_share.start()

    row_of = lax.broadcasted_iota(jnp.int32, (rows, rows), 0)
    col_of = lax.broadcasted_iota(jnp.int32, (rows, rows), 1)
    bias[...] = jnp.where(lax.rem(row_of, group) == lax.rem(col_of, group), 0.0, -1e30)

    @pl.when(y != 0)
    def _():
        w_first.wait()

    @pl.when(y == 0)
    def _():
        w_own.wait()

    w_second = [
        remote(
            w_rec.at[core, x_lo, slot],
            w_rec.at[core, x_lo, slot],
            w_send.at[1],
            w_recv.at[1],
            at(y_=lax.rem(y + step, n_y)),
        )
        for step in range(1, n_y)
    ]
    for copy in w_second:
        copy.start()
    z_half = n_z // 2
    low, high = pl.ds(0, z_half), pl.ds(z_half, n_z - z_half)
    mine = w_rec.at[core, x_lo]
    w_third = (
        remote(mine.at[low], mine.at[low], w_send.at[2], w_recv.at[2], ahead),
        remote(mine.at[high], mine.at[high], w_send.at[3], w_recv.at[3], behind),
    )
    w_fourth = remote(w_rec.at[core], w_rec.at[core], w_send.at[4], w_recv.at[4], sibling)

    def wait_second():
        whole = w_rec.at[core, x_lo, pl.ds(0, n_y - 1)]
        copy = remote(whole, whole, w_send.at[1], w_recv.at[1], sibling)
        copy.wait_send()
        copy.wait_recv()

    wait_second()
    for copy in w_third:
        copy.start()

    def to_rows(dst, src):
        dst[...] = src[...].astype(F32).reshape(rows, width).astype(BF16)

    def cut(ref, h):
        return ref[:, h * head : (h + 1) * head]

    def softmax(h):
        score = dot(cut(k_rows, h), cut(q_rows, h), NT) + bias[...]
        top = jnp.max(score, axis=0, keepdims=True)
        grown = jnp.exp((score - top) * scale)
        probs[h] = grown * (1.0 / jnp.sum(grown, axis=0, keepdims=True))

    arrive(0, q_in, q_rec)
    arrive(1, k_in, k_rec)
    to_rows(q_rows, q_rec)
    to_rows(k_rows, k_rec)
    for h in range(HEADS // 2):
        softmax(h)
    for copy in w_third:
        copy.wait()
    w_fourth.start()
    for h in range(HEADS // 2, HEADS):
        softmax(h)
    w_fourth.wait()

    quad = 4 * own_rows
    for b in range(peers // 4):
        parts = []
        for s in range(4 * b, 4 * b + 4):
            parts.append(w_rec[s % 2, s // (2 * n_z), (s // 2) % n_z].astype(F32))
        w_full[b * quad : (b + 1) * quad, :] = jnp.concatenate(parts, axis=0).astype(BF16)
    d_att[...] = dot(d_mixed, w_full[...], NN).astype(BF16)
    for h in range(HEADS):
        wide[:, h * head : (h + 1) * head] = dot(probs[h].astype(BF16), cut(d_att, h), NN)
    gv_send[...] = wide[...].reshape(peers, group, width).astype(BF16)
    spread(3, gv_send, gv_out)

    arrive(2, v_in, v_rec)
    to_rows(v_rows, v_rec)
    for h in range(HEADS):
        wide[:, h * head : (h + 1) * head] = dot(probs[h].astype(BF16), cut(v_rows, h), TN)
    att[...] = wide[...].astype(BF16)
    att_share = remote(att, att_sib, sib_send.at[1], sib_recv.at[1], sibling)
    att_share.start()

    dm_share.wait_recv()
    for b in range(4):
        x_own[b] = dot(dm_rows[core, b], att[...], NN)
    att_share.wait_recv()
    inverse_root = 1.0 / math.sqrt(tokens)
    for b in range(4):
        total = (x_own[b] + dot(dm_sib[b], att_sib[...], NN)) * inverse_root
        x_own[b] = total
        x_send[b] = total.astype(BF16)
    x_copies = []
    for step in (1, 3, 2):
        to = lax.rem(x + step, 4)
        x_copies.append(
            remote(
                x_send.at[to], x_rec.at[step], x_ssem.at[step], x_rsem.at[step], at(x_=to)
            )
        )
        x_copies[-1].start()

    mixed = dot(att[...], w_full[...], NT).reshape(peers, group, width)
    branch_out[...] = (mixed * gate_in[...][None]).reshape(rows, width).astype(BF16)

    for h in range(HEADS):
        prob = probs[h]
        d_prob = dot(cut(v_rows, h), cut(d_att, h), NT)
        centre = jnp.sum(prob * d_prob, axis=0, keepdims=True)
        d_score = (prob * (d_prob - centre) * scale).astype(BF16)
        wide[:, h * head : (h + 1) * head] = dot(d_score, cut(k_rows, h), TN)
        wide2[:, h * head : (h + 1) * head] = dot(d_score, cut(q_rows, h), NN)
    gq_send[...] = wide[...].reshape(peers, group, width).astype(BF16)
    spread(4, gq_send, gq_out)
    gk_send[...] = wide2[...].reshape(peers, group, width).astype(BF16)
    spread(5, gk_send, gk_out)

    for copy in x_copies:
        copy.wait()
    total = x_own[x]
    for step in range(1, 4):
        total += x_rec[step].astype(F32)
    x_sum[...] = total
    z_send[...] = jnp.zeros_like(z_send)
    for j in range(n_z):
        z_send[j, :half, :] = x_sum[j * half : (j + 1) * half, :].astype(BF16)
    for step in range(1, n_z):
        to = lax.rem(z + step, n_z)
        remote(z_send.at[to], z_rec.at[z], r_send.at[0], r_recv.at[0], at(z_=to)).start()
    z_rec[z] = z_send[z]
    z_all = remote(
        z_send.at[pl.ds(0, n_z - 1)],
        z_rec.at[pl.ds(0, n_z - 1)],
        r_send.at[0],
        r_recv.at[0],
        sibling,
    )
    z_all.wait_recv()

    total = z_rec[0].astype(F32)
    for j in range(1, n_z):
        total += z_rec[j].astype(F32)
    y_rec[y] = total.astype(BF16)
    for step in range(1, n_y):
        remote(
            y_rec.at[y],
            y_rec.at[y],
            r_send.at[1],
            r_recv.at[1],
            at(y_=lax.rem(y + step, n_y)),
        ).start()
    y_part = y_rec.at[pl.ds(0, n_y - 1)]
    y_all = remote(y_part, y_part, r_send.at[1], r_recv.at[1], sibling)
    y_all.wait_recv()
    total = y_rec[0].astype(F32)
    for j in range(1, n_y):
        total += y_rec[j].astype(F32)
    fin[x_hi] = total
    last = remote(
        fin.at[x_hi], fin.at[x_hi], r_send.at[2], r_recv.at[2], at(x_=lax.rem(x + 2, 4))
    )
    last.start()
    last.wait()
    gw_out[:half, :] = fin[0, :half, :]
    gw_out[half:, :] = fin[1, :half, :]

    arrive(3, gv_send, gv_out)
    arrive(4, gq_send, gq_out)
    arrive(5, gk_send, gk_out)
    sent(0, q_in, q_rec)
    sent(1, k_in, k_rec)
    sent(2, v_in, v_rec)
    sent(3, gv_send, gv_out)
    sent(4, gq_send, gq_out)
    sent(5, gk_send, gk_out)
    dm_share.wait_send()
    att_share.wait_send()
    z_all.wait_send()
    y_all.wait_send()


def body(n_y, n_z, tokens, queries, key_states, value_states, gate_vector, out_weight, cotangent):
    clips, frames, patches, width = cotangent.shape
    group, rows = clips * patches, clips * patches * frames
    own_rows = out_weight.shape[0]
    half = own_rows // 2
    block = n_z * half

    def planes(t):
        return (
            t.reshape(clips, frames, patches, width)
            .transpose(1, 0, 2, 3)
            .reshape(frames, group, width)
        )

    d_mixed = (
        (planes(cotangent).astype(F32).reshape(frames, clips, patches, width)
         * gate_vector[None, :, None, :])
        .astype(BF16)
        .reshape(rows, width)
    )
    gate_rows = jnp.repeat(gate_vector, patches, axis=0)
    plane = jax.ShapeDtypeStruct((frames, group, width), BF16)
    vmem = pl.BlockSpec(memory_space=pltpu.VMEM)
    flat = pltpu.VMEM((rows, width), BF16)
    flat32 = pltpu.VMEM((rows, width), F32)
    stack = pltpu.VMEM((frames, group, width), BF16)
    dma = pltpu.SemaphoreType.DMA
    branch, gq, gk, gv, gw = pl.pallas_call(
        functools.partial(kernel, n_y, n_z, tokens),
        out_shape=[
            jax.ShapeDtypeStruct((rows, width), BF16),
            plane,
            plane,
            plane,
            jax.ShapeDtypeStruct((own_rows, width), F32),
        ],
        in_specs=[vmem] * 6,
        out_specs=[vmem] * 5,
        scratch_shapes=[
            stack,
            stack,
            stack,
            flat,
            flat,
            flat,
            pltpu.VMEM((2, 2, n_z, own_rows, width), BF16),
            pltpu.VMEM((width, width), BF16),
            pltpu.VMEM((rows, rows), F32),
            pltpu.VMEM((HEADS, rows, rows), F32),
            flat,
            flat32,
            flat32,
            stack,
            stack,
            stack,
            pltpu.VMEM((2, 4, block, rows), BF16),
            pltpu.VMEM((4, block, rows), BF16),
            flat,
            flat,
            pltpu.VMEM((4, block, width), F32),
            pltpu.VMEM((4, block, width), BF16),
            pltpu.VMEM((4, block, width), BF16),
            pltpu.VMEM((block, width), F32),
            pltpu.VMEM((n_z, up8(half), width), BF16),
            pltpu.VMEM((n_z, up8(half), width), BF16),
            pltpu.VMEM((n_y, up8(half), width), BF16),
            pltpu.VMEM((2, up8(half), width), F32),
            dma((6,)),
            dma((6,)),
            dma((6,)),
            dma((5,)),
            dma((6,)),
            dma((2,)),
            dma((2,)),
            dma((4,)),
            dma((4,)),
            dma((3,)),
            dma((3,)),
        ],
        compiler_params=pltpu.CompilerParams(
            collective_id=1, has_side_effects=True, vmem_limit_bytes=56 << 20
        ),
    )(planes(queries), planes(key_states), planes(value_states), d_mixed, gate_rows, out_weight)

    def by_clip(t):
        return t.reshape(frames, clips, patches, width).transpose(1, 0, 2, 3)

    def home(t):
        return by_clip(t).reshape(queries.shape)

    return by_clip(branch), home(gq), home(gk), home(gv), gw


def solution(mesh):
    n_dp, n_seq = mesh.shape["dp"], mesh.shape["seq"]

    def step(queries, key_states, value_states, gate_vector, out_weight, cotangent):
        clips, frames, patches, _ = cotangent.shape
        tokens = clips * frames * patches * n_dp * n_seq
        return body(
            n_dp // 2,
            n_seq // 4,
            tokens,
            queries,
            key_states,
            value_states,
            gate_vector,
            out_weight,
            cotangent,
        )

    framed = P("dp", "seq", None, None)
    patched = P("dp", None, "seq", None)
    return jax.shard_map(
        step,
        mesh=mesh,
        in_specs=(framed, framed, framed, P("dp", None), P("seq", None), patched),
        out_specs=(patched, framed, framed, framed, P("seq", None)),
        check_vma=False,
    )
```

time: 479 us -> 149 us (0.31)
  the two profiles are of different devices: /device:TPU:64 before, /device:TPU:70 now
where the time goes in v2:
time: 149 us; the launch traced here: 148 us
  Pallas kernels  132 us (89%)
  local copies, waits for them, and re-layouts  15.7 us (11%)
    pallas_call x1, Pallas kernels, body(): pl.pallas_call(functools.partial(kernel, n_y, n_z, tokens), out_shape=[ja...  132 us

profile of v2, /device:TPU:70, one launch (start us, length us, event | category | flops | bytes accessed | tf_op | source)
XLA Modules:
  0.0 148.3 jit_solution(11486317968566413866)
XLA Ops:
  0.6 0.7 broadcast_in_dim.4
  1.3 0.6 reshape.65.gate_in
  2.0 1.5 %reshape.58 = bf16[2,32,4,1152]{3,2,1,0:T(4,128)(2,1)S(1)} reshape(bf16[2,1,128,1152]{3,2,1,0:T(8,128)(2,1)} %param.6) | data formatting | bytes 1179648 | tf_op jit(solution)/shard_map/reshape | solution.py:393
  3.5 0.2 copy.26
  3.7 1.0 reshape.59.q_in
  5.0 0.2 copy.25
  5.2 1.0 reshape.61.k_in
  6.2 0.2 copy-done.1
  6.5 0.2 copy.24
  6.7 1.0 reshape.63.v_in
  7.7 0.2 fusion
  8.0 0.2 copy.14
  8.2 1.0 reshape.64.dm_in
  9.1 131.6 %shard_map.101 = (bf16[256,1152]{1,0:T(8,128)(2,1)}, bf16[32,8,1152]{2,1,0:T(8,128)(2,1)}, bf16[32,8,1152]{2,1,0:T(8,128)(2,1)}, bf16[32,8,1152]{2,1,0:T(8,128)(2,1)}, f32[36,1152]{1,0:T(8,128)}) custom-call(bf16[32,8,1152]{2,1,0:T(8,128)(2,1)} %reshape.59.q_in, bf16[32,8,1152]{2,1,0:T(8,128)(2,1)} %reshape.61.k_in, bf16[32,8,1152]{2,1,0:T(8,128)(2,1)} %reshape.63.v_in, ...), custom_call_target="tpu_custom_call" | custom-call | tf_op jit(solution)/shard_map/pallas_call | solution.py:411
  140.7 1.5 %reshape.66 = bf16[32,2,4,1152]{3,2,1,0:T(4,128)(2,1)S(1)} reshape(bf16[256,1152]{1,0:T(8,128)(2,1)} %get-tuple-element.10) | data formatting | bytes 1179648 | tf_op jit(solution)/shard_map/reshape | solution.py:469
  142.3 1.0 copy.23
  143.5 0.2 copy.16
  143.7 1.0 reshape.68
  144.7 0.2 copy-done.3
  145.0 0.2 copy.17
  145.2 1.0 reshape.70
  146.4 0.2 copy.18
  146.7 1.0 reshape.72
  147.6 0.7 copy.28
  (19 shorter events, 1.1 us)
Async XLA Ops:
  3.7 1.1 copy-start
  5.2 1.1 copy-start.1
  6.7 1.1 copy-start.5
  6.7 1.1 copy-start.7
  142.3 1.1 copy-start.4
  143.7 1.1 copy-start.3
  145.2 1.1 copy-start.2
  146.6 1.0 copy-start.6

commit v3 on v2

--- a/solution.py
+++ b/solution.py
@@ -32,7 +32,7 @@
     q_in,
     k_in,
     v_in,
-    dm_in,
+    cot_in,
     gate_in,
     w_in,
     branch_out,
@@ -40,6 +40,10 @@
     gk_out,
     gv_out,
     gw_out,
+    q_pl,
+    k_pl,
+    v_pl,
+    d_mix,
     q_rec,
     k_rec,
     v_rec,
@@ -73,6 +77,8 @@
     a2a_own,
     w_send,
     w_recv,
+    wy_recv,
+    wx_recv,
     sib_send,
     sib_recv,
     x_ssem,
@@ -80,7 +86,7 @@
     r_send,
     r_recv,
 ):
-    peers, group, width = q_in.shape
+    peers, group, width = q_rec.shape
     rows = peers * group
     head = width // HEADS
     scale = 1.0 / math.sqrt(head)
@@ -135,7 +141,7 @@
         w_recv.at[0],
         at(z_=lax.rem(z - y + n_z, n_z)),
     )
-    w_own = pltpu.make_async_copy(w_in, w_rec.at[core, x_lo, z], w_recv.at[5])
+    w_own = pltpu.make_async_copy(w_in, w_rec.at[core, x_lo, z], w_recv.at[2])
 
     @pl.when(y != 0)
     def _():
@@ -145,7 +151,7 @@
     def _():
         w_own.start()
 
-    def spread(t, src, dst):
+    def spread(t, src, dst, first=1, last=None):
         def send(step, carry):
             target = lax.rem(seq + step, peers)
             remote(
@@ -153,8 +159,9 @@
             ).start()
             return carry
 
-        lax.fori_loop(1, peers, send, 0)
-        pltpu.make_async_copy(src.at[seq], dst.at[seq], a2a_own.at[t]).start()
+        lax.fori_loop(first, last or peers, send, 0)
+        if first == 1:
+            pltpu.make_async_copy(src.at[seq], dst.at[seq], a2a_own.at[t]).start()
 
     def arrive(t, src, dst):
         remote(
@@ -175,12 +182,30 @@
             sibling,
         ).wait_send()
 
-    spread(0, q_in, q_rec)
-    spread(1, k_in, k_rec)
-    spread(2, v_in, v_rec)
+    def deal(src, dst):
+        first = src[0, 0].astype(F32).reshape(peers // 2, group, width)
+        second = src[1, 0].astype(F32).reshape(peers // 2, group, width)
+        each = group // 2
+        even = jnp.concatenate([first[:, :each], second[:, :each]], axis=1)
+        odd = jnp.concatenate([first[:, each:], second[:, each:]], axis=1)
+        both = jnp.stack([even, odd], axis=1).reshape(peers, group, width)
+        dst[...] = both.astype(BF16)
+
+    deal(q_in, q_pl)
+    spread(0, q_pl, q_rec)
+    deal(k_in, k_pl)
+    spread(1, k_pl, k_rec)
+    deal(v_in, v_pl)
+    spread(2, v_pl, v_rec)
+
+    gate = jnp.concatenate(
+        [jnp.broadcast_to(gate_in[c : c + 1, :], (group // 2, width)) for c in range(2)], axis=0
+    )
+    cot = jnp.concatenate([cot_in[0].astype(F32), cot_in[1].astype(F32)], axis=1)
+    d_mix[...] = (cot * gate[None]).reshape(rows, width).astype(BF16)
 
     block = n_z * half
-    d_mixed = dm_in[...]
+    d_mixed = d_mix[...]
     row = lax.broadcasted_iota(jnp.int32, (block, 1), 0)
     turn = sum((row >= half * j).astype(jnp.int32) for j in range(1, n_z))
     row = row + turn * (2 * own_rows - half)
@@ -207,36 +232,40 @@
     def _():
         w_own.wait()
 
-    w_second = [
+    order = [1, 7, 2, 6, 3, 5, 4][:n_y - 1] if n_y == 8 else list(range(1, n_y))
+
+    def shard(step, x_lo_):
+        return w_rec.at[core, x_lo_, lax.rem(z + y - step + n_z, n_z)]
+
+    def hop(step, x_lo_, send, recv, to):
+        return remote(shard(step, x_lo_), shard(step, x_lo_), send, recv, to)
+
+    def along_y(step):
+        return hop(step, x_lo, w_send.at[1], wy_recv.at[step], sibling)
+
+    def along_x(step, turn, x_lo_):
+        to = ahead if turn % 2 else behind
+        return hop(step, x_lo_, w_send.at[2], wx_recv.at[step], to)
+
+    def across(step, x_lo_):
+        return hop(step, x_lo_, w_send.at[3], w_recv.at[1], sibling)
+
+    for step in order:
         remote(
-            w_rec.at[core, x_lo, slot],
-            w_rec.at[core, x_lo, slot],
+            shard(0, x_lo),
+            shard(0, x_lo),
             w_send.at[1],
-            w_recv.at[1],
+            wy_recv.at[step],
             at(y_=lax.rem(y + step, n_y)),
-        )
-        for step in range(1, n_y)
-    ]
-    for copy in w_second:
-        copy.start()
-    z_half = n_z // 2
-    low, high = pl.ds(0, z_half), pl.ds(z_half, n_z - z_half)
-    mine = w_rec.at[core, x_lo]
-    w_third = (
-        remote(mine.at[low], mine.at[low], w_send.at[2], w_recv.at[2], ahead),
-        remote(mine.at[high], mine.at[high], w_send.at[3], w_recv.at[3], behind),
-    )
-    w_fourth = remote(w_rec.at[core], w_rec.at[core], w_send.at[4], w_recv.at[4], sibling)
-
-    def wait_second():
-        whole = w_rec.at[core, x_lo, pl.ds(0, n_y - 1)]
-        copy = remote(whole, whole, w_send.at[1], w_recv.at[1], sibling)
-        copy.wait_send()
-        copy.wait_recv()
-
-    wait_second()
-    for copy in w_third:
-        copy.start()
+        ).start()
+    for turn, step in enumerate([0] + order):
+        if step:
+            along_y(step).wait_recv()
+        along_x(step, turn, x_lo).start()
+        across(step, x_lo).start()
+    for turn, step in enumerate([0] + order):
+        along_x(step, turn, 1 - x_lo).wait_recv()
+        across(step, 1 - x_lo).start()
 
     def to_rows(dst, src):
         dst[...] = src[...].astype(F32).reshape(rows, width).astype(BF16)
@@ -250,18 +279,15 @@
         grown = jnp.exp((score - top) * scale)
         probs[h] = grown * (1.0 / jnp.sum(grown, axis=0, keepdims=True))
 
-    arrive(0, q_in, q_rec)
-    arrive(1, k_in, k_rec)
+    arrive(0, q_pl, q_rec)
+    arrive(1, k_pl, k_rec)
     to_rows(q_rows, q_rec)
     to_rows(k_rows, k_rec)
-    for h in range(HEADS // 2):
+    for h in range(HEADS):
         softmax(h)
-    for copy in w_third:
-        copy.wait()
-    w_fourth.start()
-    for h in range(HEADS // 2, HEADS):
-        softmax(h)
-    w_fourth.wait()
+    remote(
+        w_rec.at[core], w_rec.at[1 - core], w_send.at[3], w_recv.at[1], sibling
+    ).wait_recv()
 
     quad = 4 * own_rows
     for b in range(peers // 4):
@@ -269,13 +295,13 @@
         for s in range(4 * b, 4 * b + 4):
             parts.append(w_rec[s % 2, s // (2 * n_z), (s // 2) % n_z].astype(F32))
         w_full[b * quad : (b + 1) * quad, :] = jnp.concatenate(parts, axis=0).astype(BF16)
-    d_att[...] = dot(d_mixed, w_full[...], NN).astype(BF16)
+    d_att[...] = dot(d_mix[...], w_full[...], NN).astype(BF16)
     for h in range(HEADS):
         wide[:, h * head : (h + 1) * head] = dot(probs[h].astype(BF16), cut(d_att, h), NN)
     gv_send[...] = wide[...].reshape(peers, group, width).astype(BF16)
     spread(3, gv_send, gv_out)
 
-    arrive(2, v_in, v_rec)
+    arrive(2, v_pl, v_rec)
     to_rows(v_rows, v_rec)
     for h in range(HEADS):
         wide[:, h * head : (h + 1) * head] = dot(probs[h].astype(BF16), cut(v_rows, h), TN)
@@ -303,7 +329,9 @@
         x_copies[-1].start()
 
     mixed = dot(att[...], w_full[...], NT).reshape(peers, group, width)
-    branch_out[...] = (mixed * gate_in[...][None]).reshape(rows, width).astype(BF16)
+    mixed = (mixed * gate[None]).astype(BF16)
+    for c in range(2):
+        branch_out[c] = mixed[:, c * (group // 2) : (c + 1) * (group // 2), :]
 
     for h in range(HEADS):
         prob = probs[h]
@@ -315,7 +343,7 @@
     gq_send[...] = wide[...].reshape(peers, group, width).astype(BF16)
     spread(4, gq_send, gq_out)
     gk_send[...] = wide2[...].reshape(peers, group, width).astype(BF16)
-    spread(5, gk_send, gk_out)
+    spread(5, gk_send, gk_out, 1, peers // 2)
 
     for copy in x_copies:
         copy.wait()
@@ -329,6 +357,7 @@
     for step in range(1, n_z):
         to = lax.rem(z + step, n_z)
         remote(z_send.at[to], z_rec.at[z], r_send.at[0], r_recv.at[0], at(z_=to)).start()
+    spread(5, gk_send, gk_out, peers // 2, peers)
     z_rec[z] = z_send[z]
     z_all = remote(
         z_send.at[pl.ds(0, n_z - 1)],
@@ -369,16 +398,77 @@
     arrive(3, gv_send, gv_out)
     arrive(4, gq_send, gq_out)
     arrive(5, gk_send, gk_out)
-    sent(0, q_in, q_rec)
-    sent(1, k_in, k_rec)
-    sent(2, v_in, v_rec)
+    sent(0, q_pl, q_rec)
+    sent(1, k_pl, k_rec)
+    sent(2, v_pl, v_rec)
     sent(3, gv_send, gv_out)
     sent(4, gq_send, gq_out)
     sent(5, gk_send, gk_out)
+    row_sent = w_rec.at[core, x_lo, pl.ds(0, n_y - 1)]
+    remote(row_sent, row_sent, w_send.at[1], w_recv.at[1], sibling).wait_send()
+    all_sent = w_rec.at[core, x_lo]
+    remote(all_sent, all_sent, w_send.at[2], w_recv.at[1], sibling).wait_send()
+    remote(w_rec.at[core], w_rec.at[core], w_send.at[3], w_recv.at[1], sibling).wait_send()
     dm_share.wait_send()
     att_share.wait_send()
     z_all.wait_send()
     y_all.wait_send()
+
+
+def settle(
+    branch_in,
+    gq_in,
+    gk_in,
+    gv_in,
+    gw_in,
+    branch_out,
+    gq_out,
+    gk_out,
+    gv_out,
+    gw_out,
+    gq_pl,
+    gk_pl,
+    gv_pl,
+    gq_own,
+    gk_own,
+    gv_own,
+    branch_own,
+    gw_own,
+    sem,
+):
+    copies = [
+        pltpu.make_async_copy(src, dst, sem.at[i])
+        for i, (src, dst) in enumerate(
+            (
+                (gv_in, gv_pl),
+                (gq_in, gq_pl),
+                (gk_in, gk_pl),
+                (branch_in, branch_own),
+                (gw_in, gw_own),
+            )
+        )
+    ]
+    for copy in copies:
+        copy.start()
+    triples = ((gv_pl, gv_own, gv_out), (gq_pl, gq_own, gq_out), (gk_pl, gk_own, gk_out))
+    for i, (src, own, dst) in enumerate(triples):
+        peers, group, width = src.shape
+        each = group // 2
+        copies[i].wait()
+        pairs = src[...].astype(F32).reshape(peers // 2, 2, group, width)
+        even, odd = pairs[:, 0], pairs[:, 1]
+        for c in range(2):
+            part = slice(c * each, (c + 1) * each)
+            both = jnp.concatenate([even[:, part], odd[:, part]], axis=1)
+            own[c, 0] = both.reshape(peers * each, width).astype(BF16)
+        copies.append(pltpu.make_async_copy(own, dst, sem.at[5 + i]))
+        copies[-1].start()
+    for i, (own, dst) in ((3, (branch_own, branch_out)), (4, (gw_own, gw_out))):
+        copies[i].wait()
+        copies.append(pltpu.make_async_copy(own, dst, sem.at[5 + i]))
+        copies[-1].start()
+    for copy in copies[5:]:
+        copy.wait()
 
 
 def body(n_y, n_z, tokens, queries, key_states, value_states, gate_vector, out_weight, cotangent):
@@ -388,20 +478,6 @@
     half = own_rows // 2
     block = n_z * half
 
-    def planes(t):
-        return (
-            t.reshape(clips, frames, patches, width)
-            .transpose(1, 0, 2, 3)
-            .reshape(frames, group, width)
-        )
-
-    d_mixed = (
-        (planes(cotangent).astype(F32).reshape(frames, clips, patches, width)
-         * gate_vector[None, :, None, :])
-        .astype(BF16)
-        .reshape(rows, width)
-    )
-    gate_rows = jnp.repeat(gate_vector, patches, axis=0)
     plane = jax.ShapeDtypeStruct((frames, group, width), BF16)
     vmem = pl.BlockSpec(memory_space=pltpu.VMEM)
     flat = pltpu.VMEM((rows, width), BF16)
@@ -411,7 +487,7 @@
     branch, gq, gk, gv, gw = pl.pallas_call(
         functools.partial(kernel, n_y, n_z, tokens),
         out_shape=[
-            jax.ShapeDtypeStruct((rows, width), BF16),
+            jax.ShapeDtypeStruct(cotangent.shape, BF16),
             plane,
             plane,
             plane,
@@ -420,6 +496,10 @@
         in_specs=[vmem] * 6,
         out_specs=[vmem] * 5,
         scratch_shapes=[
+            stack,
+            stack,
+            stack,
+            flat,
             stack,
             stack,
             stack,
@@ -451,8 +531,10 @@
             dma((6,)),
             dma((6,)),
             dma((6,)),
-            dma((5,)),
-            dma((6,)),
+            dma((4,)),
+            dma((3,)),
+            dma((n_y,)),
+            dma((n_y,)),
             dma((2,)),
             dma((2,)),
             dma((4,)),
@@ -463,15 +545,34 @@
         compiler_params=pltpu.CompilerParams(
             collective_id=1, has_side_effects=True, vmem_limit_bytes=56 << 20
         ),
-    )(planes(queries), planes(key_states), planes(value_states), d_mixed, gate_rows, out_weight)
-
-    def by_clip(t):
-        return t.reshape(frames, clips, patches, width).transpose(1, 0, 2, 3)
-
-    def home(t):
-        return by_clip(t).reshape(queries.shape)
-
-    return by_clip(branch), home(gq), home(gk), home(gv), gw
+    )(queries, key_states, value_states, cotangent, gate_vector, out_weight)
+
+    whole = pl.BlockSpec(memory_space=pltpu.HBM)
+    own = pltpu.VMEM(queries.shape, BF16)
+    return pl.pallas_call(
+        settle,
+        out_shape=[
+            jax.ShapeDtypeStruct(branch.shape, branch.dtype),
+            jax.ShapeDtypeStruct(queries.shape, BF16),
+            jax.ShapeDtypeStruct(queries.shape, BF16),
+            jax.ShapeDtypeStruct(queries.shape, BF16),
+            jax.ShapeDtypeStruct(gw.shape, gw.dtype),
+        ],
+        in_specs=[whole] * 5,
+        out_specs=[whole] * 5,
+        scratch_shapes=[
+            stack,
+            stack,
+            stack,
+            own,
+            own,
+            own,
+            pltpu.VMEM(branch.shape, branch.dtype),
+            pltpu.VMEM(gw.shape, gw.dtype),
+            dma((10,)),
+        ],
+        compiler_params=pltpu.CompilerParams(vmem_limit_bytes=60 << 20),
+    )(branch, gq, gk, gv, gw)
 
 
 def solution(mesh):

time: 149 us -> 130 us (0.87)
  the two profiles are of different devices: /device:TPU:70 before, /device:TPU:2 now
where the time goes in v3:
time: 130 us; the launch traced here: 129 us
  Pallas kernels  129 us (99%)
    pallas_call x1, Pallas kernels, body(): pl.pallas_call(functools.partial(kernel, n_y, n_z, tokens), out_shape=[ja...  126 us
    pallas_call x1, Pallas kernels, body(): pl.pallas_call(settle, out_shape=[jax.ShapeDtypeStruct(branch.shape, bran...  2.75 us

profile of v3, /device:TPU:2, one launch (start us, length us, event | category | flops | bytes accessed | tf_op | source)
XLA Modules:
  0.0 129.4 jit_solution(12834752562862791648)
XLA Ops:
  0.6 125.9 %shard_map.101 = (bf16[2,32,4,1152]{3,2,1,0:T(4,128)(2,1)}, bf16[32,8,1152]{2,1,0:T(8,128)(2,1)}, bf16[32,8,1152]{2,1,0:T(8,128)(2,1)}, bf16[32,8,1152]{2,1,0:T(8,128)(2,1)}, f32[36,1152]{1,0:T(8,128)}) custom-call(bf16[2,1,128,1152]{3,2,1,0:T(8,128)(2,1)} %q_in.1, bf16[2,1,128,1152]{3,2,1,0:T(8,128)(2,1)} %k_in.1, bf16[2,1,128,1152]{3,2,1,0:T(8,128)(2,1)} %v_in.1, ...), custom_call_target="tpu_custom_call" | custom-call | tf_op jit(solution)/shard_map/pallas_call | solution.py:487
  126.5 2.7 %shard_map.102 = (bf16[2,32,4,1152]{3,2,1,0:T(4,128)(2,1)}, bf16[2,1,128,1152]{3,2,1,0:T(8,128)(2,1)}, bf16[2,1,128,1152]{3,2,1,0:T(8,128)(2,1)}, bf16[2,1,128,1152]{3,2,1,0:T(8,128)(2,1)}, f32[36,1152]{1,0:T(8,128)}) custom-call(bf16[2,32,4,1152]{3,2,1,0:T(4,128)(2,1)} %get-tuple-element.10.branch_in, bf16[32,8,1152]{2,1,0:T(8,128)(2,1)} %get-tuple-element.11.gq_in, ...), custom_call_target="tpu_custom_call" | custom-call | tf_op jit(solution)/shard_map/pallas_call | solution.py:552

commit v4 on v3

--- a/solution.py
+++ b/solution.py
@@ -62,15 +62,25 @@
     gv_send,
     dm_rows,
     dm_sib,
-    att,
-    att_sib,
-    x_own,
-    x_send,
-    x_rec,
-    x_sum,
-    z_send,
-    z_rec,
-    y_rec,
+    p_turn,
+    att_l,
+    att_r,
+    att_l_sib,
+    att_r_sib,
+    dn_rows,
+    dn_sib,
+    a_own,
+    a_send,
+    a_rec,
+    a_part,
+    a_got,
+    b_own,
+    b_send,
+    b_rec,
+    b_part,
+    b_got,
+    c_send,
+    c_rec,
     fin,
     a2a_send,
     a2a_recv,
@@ -81,10 +91,11 @@
     wx_recv,
     sib_send,
     sib_recv,
-    x_ssem,
-    x_rsem,
+    a_ssem,
+    a_rsem,
     r_send,
     r_recv,
+    fin_recv,
 ):
     peers, group, width = q_rec.shape
     rows = peers * group
@@ -127,11 +138,15 @@
         return carry
 
     lax.fori_loop(1, peers, greet_seq, 0)
-    for step in range(1, n_y):
-        greet(at(y_=lax.rem(y + step, n_y)))
-    greet(at(x_=2 * (1 - x_hi)))
-    greet(at(x_=2 * (1 - x_hi) + 1))
-    pl.semaphore_wait(barrier, peers - 1 + n_y - 1 + 2)
+    n_dp = 2 * n_y
+
+    def greet_dp(step, carry):
+        greet((lax.rem(dp + step, n_dp), seq))
+        return carry
+
+    lax.fori_loop(1, n_dp, greet_dp, 0)
+    greet(at(x_=2 * (1 - x_hi) + 1 - x_lo))
+    pl.semaphore_wait(barrier, peers + n_dp - 1)
 
     slot = lax.rem(z + y, n_z)
     w_first = remote(
@@ -198,32 +213,6 @@
     deal(v_in, v_pl)
     spread(2, v_pl, v_rec)
 
-    gate = jnp.concatenate(
-        [jnp.broadcast_to(gate_in[c : c + 1, :], (group // 2, width)) for c in range(2)], axis=0
-    )
-    cot = jnp.concatenate([cot_in[0].astype(F32), cot_in[1].astype(F32)], axis=1)
-    d_mix[...] = (cot * gate[None]).reshape(rows, width).astype(BF16)
-
-    block = n_z * half
-    d_mixed = d_mix[...]
-    row = lax.broadcasted_iota(jnp.int32, (block, 1), 0)
-    turn = sum((row >= half * j).astype(jnp.int32) for j in range(1, n_z))
-    row = row + turn * (2 * own_rows - half)
-    lane = lax.broadcasted_iota(jnp.int32, (block, width), 1)
-    for c in range(2):
-        for b in range(4):
-            first = (b % 2) * n_z * 2 * own_rows + c * own_rows + (b // 2) * half
-            pick = (lane == row + first).astype(F32).astype(BF16)
-            dm_rows[c, b] = dot(pick, d_mixed, NT).astype(BF16)
-    dm_share = remote(
-        dm_rows.at[1 - core], dm_sib, sib_send.at[0], sib_recv.at[0], sibling
-    )
-    dm_share.start()
-
-    row_of = lax.broadcasted_iota(jnp.int32, (rows, rows), 0)
-    col_of = lax.broadcasted_iota(jnp.int32, (rows, rows), 1)
-    bias[...] = jnp.where(lax.rem(row_of, group) == lax.rem(col_of, group), 0.0, -1e30)
-
     @pl.when(y != 0)
     def _():
         w_first.wait()
@@ -258,11 +247,67 @@
             wy_recv.at[step],
             at(y_=lax.rem(y + step, n_y)),
         ).start()
-    for turn, step in enumerate([0] + order):
-        if step:
-            along_y(step).wait_recv()
+    along_x(0, 0, x_lo).start()
+    across(0, x_lo).start()
+
+    gate = jnp.concatenate(
+        [jnp.broadcast_to(gate_in[c : c + 1, :], (group // 2, width)) for c in range(2)], axis=0
+    )
+    cot = jnp.concatenate([cot_in[0].astype(F32), cot_in[1].astype(F32)], axis=1)
+    d_mix[...] = (cot * gate[None]).reshape(rows, width).astype(BF16)
+    block, tall = n_z * half, 4 * half
+    far = n_z * 2 * own_rows
+
+    def picked(row, first):
+        lane = lax.broadcasted_iota(jnp.int32, (row.shape[0], width), 1)
+        pick = (lane == row + first).astype(F32).astype(BF16)
+        return dot(pick, d_mix[...], NT).astype(BF16)
+
+    def by_x(c):
+        row = lax.broadcasted_iota(jnp.int32, (block, 1), 0)
+        turn = sum((row >= half * j).astype(jnp.int32) for j in range(1, n_z))
+        row = row + turn * (2 * own_rows - half)
+        for b in range(4):
+            dm_rows[c, b] = picked(row, (b % 2) * far + c * own_rows + (b // 2) * half)
+
+    def by_z(c):
+        row = lax.broadcasted_iota(jnp.int32, (tall, 1), 0)
+        turn = sum((row >= half * j).astype(jnp.int32) for j in range(1, 4))
+        upper = (row >= half * 2).astype(jnp.int32)
+        row = row - turn * half + upper * half + (turn - 2 * upper) * far
+        for j in range(n_z):
+            dn_rows[c, j] = picked(row, j * 2 * own_rows + c * own_rows)
+
+    def clear():
+        row_of = lax.broadcasted_iota(jnp.int32, (rows, rows), 0)
+        col_of = lax.broadcasted_iota(jnp.int32, (rows, rows), 1)
+        bias[...] = jnp.where(lax.rem(row_of, group) == lax.rem(col_of, group), 0.0, -1e30)
+        a_part[...] = jnp.zeros_like(a_part)
+        b_part[...] = jnp.zeros_like(b_part)
+
+    dm_share = remote(
+        dm_rows.at[1 - core], dm_sib, sib_send.at[0], sib_recv.at[0], sibling
+    )
+    dn_share = remote(
+        dn_rows.at[1 - core], dn_sib, sib_send.at[2], sib_recv.at[2], sibling
+    )
+    chores = [
+        lambda: by_x(0),
+        lambda: by_x(1),
+        dm_share.start,
+        lambda: by_z(0),
+        lambda: by_z(1),
+        dn_share.start,
+        clear,
+    ]
+    for turn, step in enumerate(order, 1):
+        along_y(step).wait_recv()
         along_x(step, turn, x_lo).start()
         across(step, x_lo).start()
+        if chores:
+            chores.pop(0)()
+    for chore in chores:
+        chore()
     for turn, step in enumerate([0] + order):
         along_x(step, turn, 1 - x_lo).wait_recv()
         across(step, 1 - x_lo).start()
@@ -301,99 +346,186 @@
     gv_send[...] = wide[...].reshape(peers, group, width).astype(BF16)
     spread(3, gv_send, gv_out)
 
+    for h in range(HEADS):
+        p_turn[h] = probs[h].T.astype(BF16)
+
+    cols = (width // 128 + 1) // 2 * 128
+    left_heads = -(-cols // head)
+    att_shares = (
+        remote(att_l, att_l_sib, sib_send.at[1], sib_recv.at[1], sibling),
+        remote(att_r, att_r_sib, sib_send.at[3], sib_recv.at[3], sibling),
+    )
     arrive(2, v_pl, v_rec)
     to_rows(v_rows, v_rec)
-    for h in range(HEADS):
-        wide[:, h * head : (h + 1) * head] = dot(probs[h].astype(BF16), cut(v_rows, h), TN)
-    att[...] = wide[...].astype(BF16)
-    att_share = remote(att, att_sib, sib_send.at[1], sib_recv.at[1], sibling)
-    att_share.start()
-
-    dm_share.wait_recv()
-    for b in range(4):
-        x_own[b] = dot(dm_rows[core, b], att[...], NN)
-    att_share.wait_recv()
-    inverse_root = 1.0 / math.sqrt(tokens)
-    for b in range(4):
-        total = (x_own[b] + dot(dm_sib[b], att_sib[...], NN)) * inverse_root
-        x_own[b] = total
-        x_send[b] = total.astype(BF16)
-    x_copies = []
-    for step in (1, 3, 2):
-        to = lax.rem(x + step, 4)
-        x_copies.append(
-            remote(
-                x_send.at[to], x_rec.at[step], x_ssem.at[step], x_rsem.at[step], at(x_=to)
-            )
-        )
-        x_copies[-1].start()
-
-    mixed = dot(att[...], w_full[...], NT).reshape(peers, group, width)
-    mixed = (mixed * gate[None]).astype(BF16)
-    for c in range(2):
-        branch_out[c] = mixed[:, c * (group // 2) : (c + 1) * (group // 2), :]
-
-    for h in range(HEADS):
+    for h in range(left_heads):
+        wide[:, h * head : (h + 1) * head] = dot(p_turn[h], cut(v_rows, h), NN)
+    att_l[...] = wide[:, :cols].astype(BF16)
+    att_shares[0].start()
+    for h in range(left_heads, HEADS):
+        wide[:, h * head : (h + 1) * head] = dot(p_turn[h], cut(v_rows, h), NN)
+    att_r[...] = wide[:, cols:].astype(BF16)
+    att_shares[1].start()
+
+    def scored(h):
         prob = probs[h]
         d_prob = dot(cut(v_rows, h), cut(d_att, h), NT)
         centre = jnp.sum(prob * d_prob, axis=0, keepdims=True)
         d_score = (prob * (d_prob - centre) * scale).astype(BF16)
         wide[:, h * head : (h + 1) * head] = dot(d_score, cut(k_rows, h), TN)
         wide2[:, h * head : (h + 1) * head] = dot(d_score, cut(q_rows, h), NN)
+
+    ahead_heads = HEADS // 4
+    for h in range(ahead_heads):
+        scored(h)
+
+    dm_share.wait_recv()
+    dn_share.wait_recv()
+    inverse_root = 1.0 / math.sqrt(tokens)
+    att_shares[0].wait_recv()
+
+    def left(b):
+        total = dot(dm_rows[core, b], att_l[...], NN)
+        return (total + dot(dm_sib[b], att_l_sib[...], NN)) * inverse_root
+
+    def right(j):
+        total = dot(dn_rows[core, j], att_r[...], NN)
+        return ((total + dot(dn_sib[j], att_r_sib[...], NN)) * inverse_root).astype(BF16)
+
+    x_copies = {}
+
+    def send_left(step):
+        to = lax.rem(x + step, 4)
+        a_send[step] = left(to).astype(BF16)
+        x_copies[step] = remote(
+            a_send.at[step], a_rec.at[step], a_ssem.at[step], a_rsem.at[step], at(x_=to)
+        )
+        x_copies[step].start()
+
+    def send_right(step):
+        to = lax.rem(y + step, n_y)
+        b_send[step] = right(to)
+        remote(b_send.at[step], b_rec.at[y], r_send.at[0], r_recv.at[0], at(y_=to)).start()
+
+    order_y = [4, 3, 5, 2, 6, 1, 7] if n_y == 8 else list(range(1, n_y))
+    send_left(2)
+    att_shares[1].wait_recv()
+    for turn, step in enumerate(order_y):
+        if turn == 2:
+            send_left(1)
+        if turn == 4:
+            send_left(3)
+        send_right(step)
+    for step in (1, 3):
+        if step not in x_copies:
+            send_left(step)
+    a_own[...] = left(x)
+    b_rec[y] = right(y)
+
+    def settled(src, dst, count, which):
+        return remote(
+            src.at[pl.ds(0, count)],
+            dst.at[pl.ds(0, count)],
+            r_send.at[which],
+            r_recv.at[which],
+            sibling,
+        )
+
+    b_all = settled(b_send, b_rec, n_y - 1, 0)
+
+    for h in range(ahead_heads, HEADS):
+        scored(h)
     gq_send[...] = wide[...].reshape(peers, group, width).astype(BF16)
     spread(4, gq_send, gq_out)
     gk_send[...] = wide2[...].reshape(peers, group, width).astype(BF16)
     spread(5, gk_send, gk_out, 1, peers // 2)
 
-    for copy in x_copies:
-        copy.wait()
-    total = x_own[x]
+    mixed = dot(att_l[...], w_full[:, :cols], NT) + dot(att_r[...], w_full[:, cols:], NT)
+    mixed = (mixed.reshape(peers, group, width) * gate[None]).astype(BF16)
+    for c in range(2):
+        branch_out[c] = mixed[:, c * (group // 2) : (c + 1) * (group // 2), :]
+
+    for step in (1, 3, 2):
+        x_copies[step].wait()
+    total = a_own[...]
     for step in range(1, 4):
-        total += x_rec[step].astype(F32)
-    x_sum[...] = total
-    z_send[...] = jnp.zeros_like(z_send)
+        total += a_rec[step].astype(F32)
+    a_own[...] = total
     for j in range(n_z):
-        z_send[j, :half, :] = x_sum[j * half : (j + 1) * half, :].astype(BF16)
-    for step in range(1, n_z):
-        to = lax.rem(z + step, n_z)
-        remote(z_send.at[to], z_rec.at[z], r_send.at[0], r_recv.at[0], at(z_=to)).start()
+        a_part[j, :half, :] = a_own[j * half : (j + 1) * half, :].astype(BF16)
+    for step in order_y:
+        to = lax.rem(y + step, n_y)
+        remote(a_part.at[to], a_got.at[y], r_send.at[1], r_recv.at[1], at(y_=to)).start()
+    a_got[y] = a_part[y]
+    b_all.wait_recv()
+    total = b_rec[0].astype(F32)
+    for j in range(1, n_y):
+        total += b_rec[j].astype(F32)
+    b_own[...] = total
+    for b in range(4):
+        b_part[b, :half, :] = b_own[b * half : (b + 1) * half, :].astype(BF16)
+    for step in (2, 1, 3):
+        to = lax.rem(x + step, 4)
+        remote(b_part.at[to], b_got.at[x], r_send.at[2], r_recv.at[2], at(x_=to)).start()
+    b_got[x] = b_part[x]
+    b_last = settled(b_part, b_got, 3, 2)
+    a_last = settled(a_part, a_got, n_y - 1, 1)
+    b_last.wait_recv()
+    total = b_got[0].astype(F32)
+    for j in range(1, 4):
+        total += b_got[j].astype(F32)
+    c_send[:, cols:] = total.astype(BF16)
+    a_last.wait_recv()
+    total = a_got[0].astype(F32)
+    for j in range(1, n_y):
+        total += a_got[j].astype(F32)
+    c_send[:, :cols] = total.astype(BF16)
+
+    owner = y == z
+    to_owner = remote(c_send, c_rec.at[z], r_send.at[3], r_recv.at[3], at(z_=y))
+
+    @pl.when(jnp.logical_not(owner))
+    def _():
+        to_owner.start()
+
     spread(5, gk_send, gk_out, peers // 2, peers)
-    z_rec[z] = z_send[z]
-    z_all = remote(
-        z_send.at[pl.ds(0, n_z - 1)],
-        z_rec.at[pl.ds(0, n_z - 1)],
-        r_send.at[0],
-        r_recv.at[0],
-        sibling,
-    )
-    z_all.wait_recv()
-
-    total = z_rec[0].astype(F32)
-    for j in range(1, n_z):
-        total += z_rec[j].astype(F32)
-    y_rec[y] = total.astype(BF16)
-    for step in range(1, n_y):
-        remote(
-            y_rec.at[y],
-            y_rec.at[y],
-            r_send.at[1],
-            r_recv.at[1],
-            at(y_=lax.rem(y + step, n_y)),
-        ).start()
-    y_part = y_rec.at[pl.ds(0, n_y - 1)]
-    y_all = remote(y_part, y_part, r_send.at[1], r_recv.at[1], sibling)
-    y_all.wait_recv()
-    total = y_rec[0].astype(F32)
-    for j in range(1, n_y):
-        total += y_rec[j].astype(F32)
-    fin[x_hi] = total
-    last = remote(
-        fin.at[x_hi], fin.at[x_hi], r_send.at[2], r_recv.at[2], at(x_=lax.rem(x + 2, 4))
-    )
-    last.start()
-    last.wait()
-    gw_out[:half, :] = fin[0, :half, :]
-    gw_out[half:, :] = fin[1, :half, :]
+
+    def hand(step):
+        return remote(
+            fin.at[x_hi],
+            fin.at[x_hi],
+            r_send.at[4],
+            fin_recv.at[x_hi],
+            (lax.rem(dp + step, n_dp), seq),
+        )
+
+    @pl.when(owner)
+    def _():
+        c_rec[z] = c_send[...]
+        part = c_rec.at[pl.ds(0, n_z - 1)]
+        remote(part, part, r_send.at[3], r_recv.at[3], sibling).wait_recv()
+        total = c_rec[0].astype(F32)
+        for j in range(1, n_z):
+            total += c_rec[j].astype(F32)
+        fin[x_hi] = total.astype(BF16)
+
+        def send(step, carry):
+            hand(step).start()
+            return carry
+
+        lax.fori_loop(1, n_dp, send, 0)
+
+    def half_come(which):
+        part = fin.at[which]
+        return remote(part, part, r_send.at[4], fin_recv.at[which], sibling)
+
+    half_come(1 - x_hi).wait_recv()
+
+    @pl.when(jnp.logical_not(owner))
+    def _():
+        half_come(x_hi).wait_recv()
+
+    gw_out[:half, :] = fin[0].astype(F32)[:half, :]
+    gw_out[half:, :] = fin[1].astype(F32)[:half, :]
 
     arrive(3, gv_send, gv_out)
     arrive(4, gq_send, gq_out)
@@ -410,9 +542,24 @@
     remote(all_sent, all_sent, w_send.at[2], w_recv.at[1], sibling).wait_send()
     remote(w_rec.at[core], w_rec.at[core], w_send.at[3], w_recv.at[1], sibling).wait_send()
     dm_share.wait_send()
-    att_share.wait_send()
-    z_all.wait_send()
-    y_all.wait_send()
+    for copy in att_shares:
+        copy.wait_send()
+    dn_share.wait_send()
+    b_all.wait_send()
+    a_last.wait_send()
+    b_last.wait_send()
+
+    @pl.when(jnp.logical_not(owner))
+    def _():
+        to_owner.wait_send()
+
+    @pl.when(owner)
+    def _():
+        def sent_on(step, carry):
+            hand(step).wait_send()
+            return carry
+
+        lax.fori_loop(1, n_dp, sent_on, 0)
 
 
 def settle(
@@ -476,7 +623,8 @@
     group, rows = clips * patches, clips * patches * frames
     own_rows = out_weight.shape[0]
     half = own_rows // 2
-    block = n_z * half
+    block, tall, pad = n_z * half, 4 * half, up8(half)
+    cols = (width // 128 + 1) // 2 * 128
 
     plane = jax.ShapeDtypeStruct((frames, group, width), BF16)
     vmem = pl.BlockSpec(memory_space=pltpu.VMEM)
@@ -518,16 +666,26 @@
             stack,
             pltpu.VMEM((2, 4, block, rows), BF16),
             pltpu.VMEM((4, block, rows), BF16),
-            flat,
-            flat,
-            pltpu.VMEM((4, block, width), F32),
-            pltpu.VMEM((4, block, width), BF16),
-            pltpu.VMEM((4, block, width), BF16),
-            pltpu.VMEM((block, width), F32),
-            pltpu.VMEM((n_z, up8(half), width), BF16),
-            pltpu.VMEM((n_z, up8(half), width), BF16),
-            pltpu.VMEM((n_y, up8(half), width), BF16),
-            pltpu.VMEM((2, up8(half), width), F32),
+            pltpu.VMEM((HEADS, rows, rows), BF16),
+            pltpu.VMEM((rows, cols), BF16),
+            pltpu.VMEM((rows, width - cols), BF16),
+            pltpu.VMEM((rows, cols), BF16),
+            pltpu.VMEM((rows, width - cols), BF16),
+            pltpu.VMEM((2, n_z, tall, rows), BF16),
+            pltpu.VMEM((n_z, tall, rows), BF16),
+            pltpu.VMEM((block, cols), F32),
+            pltpu.VMEM((4, block, cols), BF16),
+            pltpu.VMEM((4, block, cols), BF16),
+            pltpu.VMEM((n_z, pad, cols), BF16),
+            pltpu.VMEM((n_y, pad, cols), BF16),
+            pltpu.VMEM((tall, width - cols), F32),
+            pltpu.VMEM((n_y, tall, width - cols), BF16),
+            pltpu.VMEM((n_y, tall, width - cols), BF16),
+            pltpu.VMEM((4, pad, width - cols), BF16),
+            pltpu.VMEM((4, pad, width - cols), BF16),
+            pltpu.VMEM((pad, width), BF16),
+            pltpu.VMEM((n_z, pad, width), BF16),
+            pltpu.VMEM((2, pad, width), BF16),
             dma((6,)),
             dma((6,)),
             dma((6,)),
@@ -535,12 +693,13 @@
             dma((3,)),
             dma((n_y,)),
             dma((n_y,)),
-            dma((2,)),
-            dma((2,)),
             dma((4,)),
             dma((4,)),
-            dma((3,)),
-            dma((3,)),
+            dma((4,)),
+            dma((4,)),
+            dma((5,)),
+            dma((5,)),
+            dma((2,)),
         ],
         compiler_params=pltpu.CompilerParams(
             collective_id=1, has_side_effects=True, vmem_limit_bytes=56 << 20

time: 130 us -> 115 us (0.88)
  the two profiles are of different devices: /device:TPU:2 before, /device:TPU:70 now
where the time goes in v4:
time: 115 us
  Pallas kernels  114 us (99%)
    pallas_call x1, Pallas kernels, body(): pl.pallas_call(functools.partial(kernel, n_y, n_z, tokens), out_shape=[ja...  111 us
    pallas_call x1, Pallas kernels, body(): pl.pallas_call(settle, out_shape=[jax.ShapeDtypeStruct(branch.shape, bran...  2.75 us

profile of v4, /device:TPU:70, one launch (start us, length us, event | category | flops | bytes accessed | tf_op | source)
XLA Modules:
  0.0 114.9 jit_solution(156779407560939684)
XLA Ops:
  0.6 111.3 %shard_map.101 = (bf16[2,32,4,1152]{3,2,1,0:T(4,128)(2,1)}, bf16[32,8,1152]{2,1,0:T(8,128)(2,1)}, bf16[32,8,1152]{2,1,0:T(8,128)(2,1)}, bf16[32,8,1152]{2,1,0:T(8,128)(2,1)}, f32[36,1152]{1,0:T(8,128)}) custom-call(bf16[2,1,128,1152]{3,2,1,0:T(8,128)(2,1)} %q_in.1, bf16[2,1,128,1152]{3,2,1,0:T(8,128)(2,1)} %k_in.1, bf16[2,1,128,1152]{3,2,1,0:T(8,128)(2,1)} %v_in.1, ...), custom_call_target="tpu_custom_call" | custom-call | tf_op jit(solution)/shard_map/pallas_call | solution.py:635
  111.9 2.7 %shard_map.102 = (bf16[2,32,4,1152]{3,2,1,0:T(4,128)(2,1)}, bf16[2,1,128,1152]{3,2,1,0:T(8,128)(2,1)}, bf16[2,1,128,1152]{3,2,1,0:T(8,128)(2,1)}, bf16[2,1,128,1152]{3,2,1,0:T(8,128)(2,1)}, f32[36,1152]{1,0:T(8,128)}) custom-call(bf16[2,32,4,1152]{3,2,1,0:T(4,128)(2,1)} %get-tuple-element.10.branch_in, bf16[32,8,1152]{2,1,0:T(8,128)(2,1)} %get-tuple-element.11.gq_in, ...), custom_call_target="tpu_custom_call" | custom-call | tf_op jit(solution)/shard_map/pallas_call | solution.py:711

commit v5 on v4

--- a/solution.py
+++ b/solution.py
@@ -40,6 +40,11 @@
     gk_out,
     gv_out,
     gw_out,
+    q_raw,
+    k_raw,
+    v_raw,
+    cot_raw,
+    in_sem,
     q_pl,
     k_pl,
     v_pl,
@@ -128,6 +133,15 @@
     sibling = at(core_=1 - core)
     ahead, behind = at(x_=lax.rem(x + 1, 4)), at(x_=lax.rem(x + 3, 4))
 
+    fetches = [
+        pltpu.make_async_copy(src, dst, in_sem.at[i])
+        for i, (src, dst) in enumerate(
+            ((q_in, q_raw), (k_in, k_raw), (v_in, v_raw), (cot_in, cot_raw))
+        )
+    ]
+    for copy in fetches:
+        copy.start()
+
     barrier = pltpu.get_barrier_semaphore()
 
     def greet(to):
@@ -146,6 +160,18 @@
 
     lax.fori_loop(1, n_dp, greet_dp, 0)
     greet(at(x_=2 * (1 - x_hi) + 1 - x_lo))
+    def deal(src, dst):
+        first = src[0, 0].astype(F32).reshape(peers // 2, group, width)
+        second = src[1, 0].astype(F32).reshape(peers // 2, group, width)
+        each = group // 2
+        even = jnp.concatenate([first[:, :each], second[:, :each]], axis=1)
+        odd = jnp.concatenate([first[:, each:], second[:, each:]], axis=1)
+        both = jnp.stack([even, odd], axis=1).reshape(peers, group, width)
+        dst[...] = both.astype(BF16)
+
+    for i, (raw, planes) in enumerate(((q_raw, q_pl), (k_raw, k_pl), (v_raw, v_pl))):
+        fetches[i].wait()
+        deal(raw, planes)
     pl.semaphore_wait(barrier, peers + n_dp - 1)
 
     slot = lax.rem(z + y, n_z)
@@ -197,20 +223,8 @@
             sibling,
         ).wait_send()
 
-    def deal(src, dst):
-        first = src[0, 0].astype(F32).reshape(peers // 2, group, width)
-        second = src[1, 0].astype(F32).reshape(peers // 2, group, width)
-        each = group // 2
-        even = jnp.concatenate([first[:, :each], second[:, :each]], axis=1)
-        odd = jnp.concatenate([first[:, each:], second[:, each:]], axis=1)
-        both = jnp.stack([even, odd], axis=1).reshape(peers, group, width)
-        dst[...] = both.astype(BF16)
-
-    deal(q_in, q_pl)
     spread(0, q_pl, q_rec)
-    deal(k_in, k_pl)
     spread(1, k_pl, k_rec)
-    deal(v_in, v_pl)
     spread(2, v_pl, v_rec)
 
     @pl.when(y != 0)
@@ -253,7 +267,8 @@
     gate = jnp.concatenate(
         [jnp.broadcast_to(gate_in[c : c + 1, :], (group // 2, width)) for c in range(2)], axis=0
     )
-    cot = jnp.concatenate([cot_in[0].astype(F32), cot_in[1].astype(F32)], axis=1)
+    fetches[3].wait()
+    cot = jnp.concatenate([cot_raw[0].astype(F32), cot_raw[1].astype(F32)], axis=1)
     d_mix[...] = (cot * gate[None]).reshape(rows, width).astype(BF16)
     block, tall = n_z * half, 4 * half
     far = n_z * 2 * own_rows
@@ -628,6 +643,8 @@
 
     plane = jax.ShapeDtypeStruct((frames, group, width), BF16)
     vmem = pl.BlockSpec(memory_space=pltpu.VMEM)
+    hbm = pl.BlockSpec(memory_space=pltpu.HBM)
+    own = pltpu.VMEM(queries.shape, BF16)
     flat = pltpu.VMEM((rows, width), BF16)
     flat32 = pltpu.VMEM((rows, width), F32)
     stack = pltpu.VMEM((frames, group, width), BF16)
@@ -641,9 +658,14 @@
             plane,
             jax.ShapeDtypeStruct((own_rows, width), F32),
         ],
-        in_specs=[vmem] * 6,
+        in_specs=[hbm] * 4 + [vmem] * 2,
         out_specs=[vmem] * 5,
         scratch_shapes=[
+            own,
+            own,
+            own,
+            pltpu.VMEM(cotangent.shape, BF16),
+            dma((4,)),
             stack,
             stack,
             stack,
@@ -706,8 +728,6 @@
         ),
     )(queries, key_states, value_states, cotangent, gate_vector, out_weight)
 
-    whole = pl.BlockSpec(memory_space=pltpu.HBM)
-    own = pltpu.VMEM(queries.shape, BF16)
     return pl.pallas_call(
         settle,
         out_shape=[
@@ -717,8 +737,8 @@
             jax.ShapeDtypeStruct(queries.shape, BF16),
             jax.ShapeDtypeStruct(gw.shape, gw.dtype),
         ],
-        in_specs=[whole] * 5,
-        out_specs=[whole] * 5,
+        in_specs=[hbm] * 5,
+        out_specs=[hbm] * 5,
         scratch_shapes=[
             stack,
             stack,

time: 115 us -> 114 us (level)
  no operation moved by 1% of the time
where the time goes in v5:
time: 114 us
  Pallas kernels  113 us (99%)
    pallas_call x1, Pallas kernels, body(): pl.pallas_call(functools.partial(kernel, n_y, n_z, tokens), out_shape=[ja...  111 us
    pallas_call x1, Pallas kernels, body(): pl.pallas_call(settle, out_shape=[jax.ShapeDtypeStruct(branch.shape, bran...  2.75 us

profile of v5, /device:TPU:70, one launch (start us, length us, event | category | flops | bytes accessed | tf_op | source)
XLA Modules:
  0.0 114.1 jit_solution(8174438639684755340)
XLA Ops:
  0.6 110.5 %shard_map.101 = (bf16[2,32,4,1152]{3,2,1,0:T(4,128)(2,1)}, bf16[32,8,1152]{2,1,0:T(8,128)(2,1)}, bf16[32,8,1152]{2,1,0:T(8,128)(2,1)}, bf16[32,8,1152]{2,1,0:T(8,128)(2,1)}, f32[36,1152]{1,0:T(8,128)}) custom-call(bf16[2,1,128,1152]{3,2,1,0:T(8,128)(2,1)} %q_in.1, bf16[2,1,128,1152]{3,2,1,0:T(8,128)(2,1)} %k_in.1, bf16[2,1,128,1152]{3,2,1,0:T(8,128)(2,1)} %v_in.1, ...), custom_call_target="tpu_custom_call" | custom-call | tf_op jit(solution)/shard_map/pallas_call | solution.py:652
  111.2 2.7 %shard_map.102 = (bf16[2,32,4,1152]{3,2,1,0:T(4,128)(2,1)}, bf16[2,1,128,1152]{3,2,1,0:T(8,128)(2,1)}, bf16[2,1,128,1152]{3,2,1,0:T(8,128)(2,1)}, bf16[2,1,128,1152]{3,2,1,0:T(8,128)(2,1)}, f32[36,1152]{1,0:T(8,128)}) custom-call(bf16[2,32,4,1152]{3,2,1,0:T(4,128)(2,1)} %get-tuple-element.10.branch_in, bf16[32,8,1152]{2,1,0:T(8,128)(2,1)} %get-tuple-element.11.gq_in, ...), custom_call_target="tpu_custom_call" | custom-call | tf_op jit(solution)/shard_map/pallas_call | solution.py:731
